TPU v7x, 256 devices: a whole 4x4x8 slice. The times are simulated.
256 devices in a mesh: leaf: 32 (over z, y), grid: 8 (over x, core).
Axes of the slice: x: 4, y: 4, z: 8, core: 2. Of those that a mesh axis runs over, the one named last changes fastest.
Arguments:
- top_solution: bfloat16 [4096, 256], P(('leaf', 'grid')), may hold values from -6 to 6
- right_one: bfloat16 [32, 1024, 256], P('leaf', 'grid'), may hold values from -6 to 6
- update_one: bfloat16 [32, 2048, 1024], P('leaf', None, 'grid'), may hold values from -0.125 to 0.125
- inverse_one: bfloat16 [32, 1024, 1024], P('leaf', None, 'grid'), as said below
- top_rows_one: int32 [32, 2048], P('leaf'), may hold values from 0 to 4095, as said below
- live_one: int32 [32], P('leaf'), may hold values from 512 to 1024
- right_two: bfloat16 [384, 1024, 256], P('leaf', 'grid'), may hold values from -6 to 6
- update_two: bfloat16 [384, 2048, 1024], P('leaf', None, 'grid'), may hold values from -0.125 to 0.125
- inverse_two: bfloat16 [384, 1024, 1024], P('leaf', None, 'grid'), as said below
- top_rows_two: int32 [384, 1536], P('leaf'), may hold values from 0 to 4095, as said below
- sep_rows: int32 [384, 512], P('leaf'), may hold values from 0 to 1023, as said below
- parent: int32 [384], P('leaf'), may hold values from 0 to 31, as said below
- live_two: int32 [384], P('leaf'), may hold values from 512 to 1024
Outputs:
- solution_one: bfloat16 [32, 1024, 256], P('leaf', 'grid')
- solution_two: bfloat16 [384, 1024, 256], P('leaf', 'grid')
Inputs may be any that keep to these rules, and one draw needn't show every extreme that they name: `top_rows_one`: each row lists 2048 distinct rows in increasing order. `top_rows_two`: each row lists 1536 distinct rows in increasing order. `sep_rows`: each row lists 512 distinct rows of the parent's separator in increasing order. The parent of level-two front f differs from f // 12 by at most one; in each group of 12 fronts, one of the first two has parent f // 12 - 1 and the other f // 12 + 1, where these exist. `inverse_one`: zero above the diagonal. `inverse_two`: zero above the diagonal.
All inputs are finite; a program needn't handle non-finite values.
Results may differ from a plain program's by a relative error of at most 0.0053.
Values may be sent and summed in bfloat16 or wider, within the bound.
A program may use at most 128 MiB of HBM per device.

v0:
```python
import jax
import jax.numpy as jnp
from jax import lax
from jax.sharding import PartitionSpec as P


def with_halo(value, sides, width):
    for axis, dim in sides:
        size, length = (lax.axis_size(axis), value.shape[dim])
        up = [(i, (i + 1) % size) for i in range(size - 1)]
        down = [(j, i) for i, j in up]
        last = lax.slice_in_dim(value, length - width, length, axis=dim)
        initial = lax.slice_in_dim(value, 0, width, axis=dim)
        before = lax.ppermute(last, axis, up)
        after = lax.ppermute(initial, axis, down)
        value = jnp.concatenate([before, value, after], axis=dim)
    return value


def updated_rhs(factor, gathered, right_side):
    product = jnp.einsum("cus,cur->csr", factor, gathered, preferred_element_type=jnp.float32)
    return (right_side.astype(jnp.float32) - product).astype(jnp.bfloat16)


def make_accumulate(inverse, piece):
    return jnp.einsum("ckj,ckr->cjr", inverse, piece, preferred_element_type=jnp.float32)


def masked(summed, positions, live_rows):
    keeper = positions[None, :, None] < live_rows[:, None, None]
    return jnp.where(keeper, summed, 0.0).astype(jnp.bfloat16)


def local(
    top_solution,
    right_one,
    update_one,
    inverse_one,
    top_rows_one,
    live_one,
    right_two,
    update_two,
    inverse_two,
    top_rows_two,
    sep_rows,
    parent,
    live_two,
):
    ancestors = lax.all_gather(top_solution, ("leaf", "grid"), axis=0, tiled=True)
    row_share = right_one.shape[1]
    front_rows = row_share * lax.axis_size("grid")
    positions = lax.axis_index("grid") * row_share + jnp.arange(row_share, dtype=jnp.int32)
    gathered_one = jnp.take(ancestors, top_rows_one, axis=0)
    partial_one = updated_rhs(update_one, gathered_one, right_one)
    summed_one = make_accumulate(
        inverse_one, lax.all_gather(partial_one, "grid", axis=1, tiled=True)
    )
    solution_one = masked(summed_one, positions, live_one)
    adjacent = with_halo(solution_one, (("leaf", 0),), 1)
    adjacent_full = lax.all_gather(adjacent, "grid", axis=1, tiled=True)
    leaf_index = lax.axis_index("leaf")
    neighbour = parent - leaf_index + 1
    row_picks = neighbour[:, None] * front_rows + sep_rows
    stacked = adjacent_full.reshape(adjacent_full.shape[0] * front_rows, adjacent_full.shape[2])
    parent_rows = jnp.take(stacked, row_picks, axis=0)
    from_top = jnp.take(ancestors, top_rows_two, axis=0)
    gathered_two = jnp.concatenate([from_top, parent_rows], axis=1)

    def one_front(counter, front_items):
        factor, gathered, right_side, inverse = front_items
        partial_value = updated_rhs(factor[None], gathered[None], right_side[None])
        summed = make_accumulate(
            inverse[None], lax.all_gather(partial_value, "grid", axis=1, tiled=True)
        )
        return (counter, summed[0])

    unused, summed_two = lax.scan(
        one_front, jnp.zeros((), jnp.int32), (update_two, gathered_two, right_two, inverse_two)
    )
    solution_two = masked(summed_two, positions, live_two)
    return (solution_one, solution_two)


def solution(mesh):
    in_specs = (
        P(("leaf", "grid"), None),
        P("leaf", "grid", None),
        P("leaf", None, "grid"),
        P("leaf", None, "grid"),
        P("leaf", None),
        P("leaf"),
        P("leaf", "grid", None),
        P("leaf", None, "grid"),
        P("leaf", None, "grid"),
        P("leaf", None),
        P("leaf", None),
        P("leaf"),
        P("leaf"),
    )
    out_specs = (P("leaf", "grid", None), P("leaf", "grid", None))
    return jax.shard_map(local, mesh=mesh, in_specs=in_specs, out_specs=out_specs, check_vma=False)
```

profile of v0, /device:TPU:1, one launch (start us, length us, event | category | flops | bytes accessed | tf_op | source)
XLA Modules:
  0.0 483.9 jit_solution(13959353936855515248)
XLA Ops:
  7.2 0.7 all-gather.3.cloned.1.call-update
  8.0 0.9 copy.17
  9.6 0.7 add_multiply_fusion
  10.3 0.7 and_reduce_fusion
  11.0 1.5 compare_select_fusion
  12.6 107.4 %all-gather.3.cloned.1.call-done = bf16[4096,256]{1,0:T(8,128)(2,1)} async-done(((bf16[16,256]{1,0:T(8,128)(2,1)}), bf16[4096,256]{1,0:T(8,128)(2,1)}) %all-gather.3.cloned.1.call-update) | async-done | bytes 2097168 | tf_op jit(solution)/shard_map/all_gather | solution.py:49
  120.0 10.5 %gather_fusion = bf16[2048,256]{1,0:T(8,128)(2,1)} fusion(bf16[4096,256]{1,0:T(8,128)(2,1)} %all-gather.3.cloned.1.call-done, s32[2048]{0:T(1024)S(1)} %broadcast_clamp_fusion.2), kind=kCustom, calls=%fused_computation | custom fusion | bytes 2105344 | tf_op jit(solution)/shard_map/jit(_take)/gather | solution.py:53
  130.5 2.0 fusion.13
  132.5 12.6 %all_gather.13 = bf16[1,1024,256]{1,2,0:T(8,128)(2,1)S(1)} all-gather(bf16[1,128,256]{1,2,0:T(8,128)(2,1)S(1)} %fusion.13), channel_id=1, replica_groups=mesh['leaf'=32,'grid'=8] {'grid'}, dimensions={1}, use_global_device_ids=true | all-gather | bytes 589824 | tf_op jit(solution)/shard_map/all_gather | solution.py:56
  145.1 0.3 fusion.15
  145.4 3.8 collective-permute-start
  149.2 1.3 collective-permute-start.1
  150.6 1.5 reshape.163
  152.2 2.2 collective-permute-done.1
  154.3 1.6 pad_maximum_fusion.1
  155.9 0.7 broadcast_compare_fusion
  156.6 0.6 broadcast_clamp_fusion.1
  157.2 1.5 compare_and_fusion
  158.7 0.9 broadcast_clamp_fusion
  159.6 0.7 copy.19
  160.4 73.2 %gather_fusion.1 = bf16[18432,256]{1,0:T(8,128)(2,1)} fusion(bf16[4096,256]{1,0:T(8,128)(2,1)S(1)} %copy-done.1, s32[18432]{0:T(1024)S(1)} %broadcast_clamp_fusion), kind=kCustom, calls=%fused_computation.1 | custom fusion | bytes 18948096 | tf_op jit(solution)/shard_map/jit(_take)/gather | solution.py:66
  233.6 8.4 %broadcast_select_fusion = bf16[12,1536,256]{2,1,0:T(8,128)(2,1)} fusion(bf16[12,1536,256]{2,1,0:T(8,128)(2,1)} %bitcast.76, pred[12,1536]{1,0:T(8,128)(4,1)S(1)} %copy-done.4), kind=kLoop, calls=%fused_computation.18 | loop fusion | flops 4718592 | bytes 18892800 | tf_op jit(solution)/shard_map/jit(_take)/select_n | solution.py:66
  242.0 1.7 copy.18
  243.8 25.0 %gather_fusion.2 = bf16[6144,256]{1,0:T(8,128)(2,1)} fusion(bf16[3072,256]{1,0:T(8,128)(2,1)S(1)} %bitcast.75, s32[6144]{0:T(1024)S(1)} %copy-done.3), kind=kCustom, calls=%fused_computation.2 | custom fusion | bytes 6316032 | tf_op jit(solution)/shard_map/jit(_take)/gather | solution.py:65
  268.8 3.2 broadcast_select_fusion.1
  272.0 9.2 %pad_maximum_fusion = bf16[12,2048,256]{2,1,0:T(8,128)(2,1)} fusion(bf16[12,512,256]{2,1,0:T(8,128)(2,1)S(1)} %broadcast_select_fusion.1, bf16[12,1536,256]{2,1,0:T(8,128)(2,1)} %broadcast_select_fusion), kind=kLoop, calls=%fused_computation.17 | loop fusion | flops 25165824 | bytes 25165824 | tf_op jit(solution)/shard_map/concatenate | solution.py:67
  281.2 194.6 %while.11 = (s32[]{:T(128)}, bf16[12,128,256]{2,1,0:T(8,128)(2,1)S(1)}, bf16[12,1024,128]{2,1,0:T(8,128)(2,1)}, bf16[12,128,256]{2,1,0:T(8,128)(2,1)}, bf16[12,2...) while((s32[]{:T(128)}, bf16[12,128,256]{2,1,0:T(8,128)(2,1)S(1)}, ...), condition=%wide.region_1.2_spmd.clone, body=%wide.region_0.1_spmd.sunk.clone | while | flops 201424896 | bytes 3213893 | solution.py:77
  281.2 1.7 fusion.39
  283.0 14.5 %all_gather.17 = bf16[1,1024,256]{2,1,0:T(8,128)(2,1)S(1)} all-gather(bf16[1,128,256]{2,1,0:T(8,128)(2,1)S(1)} %fusion.39), channel_id=1, replica_groups=mesh['leaf'=32,'grid'=8] {'grid'}, dimensions={1}, use_global_device_ids=true | all-gather | bytes 589824 | tf_op jit(solution)/shard_map/while/body/eval_jaxpr/all_gather | solution.py:73
  297.5 1.2 fusion.40
  298.8 1.7 fusion.39
  300.5 13.1 %all_gather.17 = bf16[1,1024,256]{2,1,0:T(8,128)(2,1)S(1)} all-gather(bf16[1,128,256]{2,1,0:T(8,128)(2,1)S(1)} %fusion.39), channel_id=1, replica_groups=mesh['leaf'=32,'grid'=8] {'grid'}, dimensions={1}, use_global_device_ids=true | all-gather | bytes 589824 | tf_op jit(solution)/shard_map/while/body/eval_jaxpr/all_gather | solution.py:73
  313.6 1.2 fusion.40
  314.9 1.7 fusion.39
  316.6 13.1 %all_gather.17 = bf16[1,1024,256]{2,1,0:T(8,128)(2,1)S(1)} all-gather(bf16[1,128,256]{2,1,0:T(8,128)(2,1)S(1)} %fusion.39), channel_id=1, replica_groups=mesh['leaf'=32,'grid'=8] {'grid'}, dimensions={1}, use_global_device_ids=true | all-gather | bytes 589824 | tf_op jit(solution)/shard_map/while/body/eval_jaxpr/all_gather | solution.py:73
  329.7 1.2 fusion.40
  331.0 1.7 fusion.39
  332.7 13.1 %all_gather.17 = bf16[1,1024,256]{2,1,0:T(8,128)(2,1)S(1)} all-gather(bf16[1,128,256]{2,1,0:T(8,128)(2,1)S(1)} %fusion.39), channel_id=1, replica_groups=mesh['leaf'=32,'grid'=8] {'grid'}, dimensions={1}, use_global_device_ids=true | all-gather | bytes 589824 | tf_op jit(solution)/shard_map/while/body/eval_jaxpr/all_gather | solution.py:73
  345.8 1.2 fusion.40
  347.1 1.7 fusion.39
  348.8 13.1 %all_gather.17 = bf16[1,1024,256]{2,1,0:T(8,128)(2,1)S(1)} all-gather(bf16[1,128,256]{2,1,0:T(8,128)(2,1)S(1)} %fusion.39), channel_id=1, replica_groups=mesh['leaf'=32,'grid'=8] {'grid'}, dimensions={1}, use_global_device_ids=true | all-gather | bytes 589824 | tf_op jit(solution)/shard_map/while/body/eval_jaxpr/all_gather | solution.py:73
  361.9 1.2 fusion.40
  363.2 1.7 fusion.39
  364.9 13.1 %all_gather.17 = bf16[1,1024,256]{2,1,0:T(8,128)(2,1)S(1)} all-gather(bf16[1,128,256]{2,1,0:T(8,128)(2,1)S(1)} %fusion.39), channel_id=1, replica_groups=mesh['leaf'=32,'grid'=8] {'grid'}, dimensions={1}, use_global_device_ids=true | all-gather | bytes 589824 | tf_op jit(solution)/shard_map/while/body/eval_jaxpr/all_gather | solution.py:73
  378.0 1.2 fusion.40
  379.3 1.7 fusion.39
  381.0 13.1 %all_gather.17 = bf16[1,1024,256]{2,1,0:T(8,128)(2,1)S(1)} all-gather(bf16[1,128,256]{2,1,0:T(8,128)(2,1)S(1)} %fusion.39), channel_id=1, replica_groups=mesh['leaf'=32,'grid'=8] {'grid'}, dimensions={1}, use_global_device_ids=true | all-gather | bytes 589824 | tf_op jit(solution)/shard_map/while/body/eval_jaxpr/all_gather | solution.py:73
  394.1 1.2 fusion.40
  395.4 1.7 fusion.39
  397.1 13.1 %all_gather.17 = bf16[1,1024,256]{2,1,0:T(8,128)(2,1)S(1)} all-gather(bf16[1,128,256]{2,1,0:T(8,128)(2,1)S(1)} %fusion.39), channel_id=1, replica_groups=mesh['leaf'=32,'grid'=8] {'grid'}, dimensions={1}, use_global_device_ids=true | all-gather | bytes 589824 | tf_op jit(solution)/shard_map/while/body/eval_jaxpr/all_gather | solution.py:73
  410.2 1.2 fusion.40
  411.5 1.7 fusion.39
  413.2 13.1 %all_gather.17 = bf16[1,1024,256]{2,1,0:T(8,128)(2,1)S(1)} all-gather(bf16[1,128,256]{2,1,0:T(8,128)(2,1)S(1)} %fusion.39), channel_id=1, replica_groups=mesh['leaf'=32,'grid'=8] {'grid'}, dimensions={1}, use_global_device_ids=true | all-gather | bytes 589824 | tf_op jit(solution)/shard_map/while/body/eval_jaxpr/all_gather | solution.py:73
  426.4 1.2 fusion.40
  427.6 1.7 fusion.39
  429.3 13.1 %all_gather.17 = bf16[1,1024,256]{2,1,0:T(8,128)(2,1)S(1)} all-gather(bf16[1,128,256]{2,1,0:T(8,128)(2,1)S(1)} %fusion.39), channel_id=1, replica_groups=mesh['leaf'=32,'grid'=8] {'grid'}, dimensions={1}, use_global_device_ids=true | all-gather | bytes 589824 | tf_op jit(solution)/shard_map/while/body/eval_jaxpr/all_gather | solution.py:73
  442.5 1.2 fusion.40
  443.7 1.7 fusion.39
  445.4 13.1 %all_gather.17 = bf16[1,1024,256]{2,1,0:T(8,128)(2,1)S(1)} all-gather(bf16[1,128,256]{2,1,0:T(8,128)(2,1)S(1)} %fusion.39), channel_id=1, replica_groups=mesh['leaf'=32,'grid'=8] {'grid'}, dimensions={1}, use_global_device_ids=true | all-gather | bytes 589824 | tf_op jit(solution)/shard_map/while/body/eval_jaxpr/all_gather | solution.py:73
  458.6 1.2 fusion.40
  459.8 1.7 fusion.39
  461.5 13.1 %all_gather.17 = bf16[1,1024,256]{2,1,0:T(8,128)(2,1)S(1)} all-gather(bf16[1,128,256]{2,1,0:T(8,128)(2,1)S(1)} %fusion.39), channel_id=1, replica_groups=mesh['leaf'=32,'grid'=8] {'grid'}, dimensions={1}, use_global_device_ids=true | all-gather | bytes 589824 | tf_op jit(solution)/shard_map/while/body/eval_jaxpr/all_gather | solution.py:73
  474.7 1.2 fusion.40
  475.9 1.2 select_convert_fusion
  (27 shorter events, 0.2 us)
Async XLA Ops:
  7.2 123.3 %copy-start = (bf16[1,2048,128]{2,1,0:T(8,128)(2,1)S(1)}, bf16[1,2048,128]{2,1,0:T(8,128)(2,1)}, u32[]{:S(2)}) copy-start(bf16[1,2048,128]{2,1,0:T(8,128)(2,1)} %param.17) | copy-start | bytes 1572868
  7.2 112.8 %all-gather.3.cloned.1.call-start = ((), (), s32[]{:S(2)}) async-start(), calls=%async_computation | async-start | bytes 2105344 | tf_op jit(solution)/shard_map/all_gather | solution.py:49
  7.9 234.1 %all-gather.5.cloned.1.call-start = ((), (), s32[]{:S(2)}) async-start(), calls=%async_computation.1 | async-start | bytes 1769472 | tf_op jit(solution)/shard_map/all_gather | solution.py:60
  12.6 132.5 %copy-start.2 = (bf16[1,1024,128]{2,1,0:T(8,128)(2,1)S(1)}, bf16[1,1024,128]{2,1,0:T(8,128)(2,1)}, u32[]{:S(2)}) copy-start(bf16[1,1024,128]{2,1,0:T(8,128)(2,1)} %param.18) | copy-start | bytes 786436
  12.6 138.0 %copy-start.5 = (s32[12,512]{1,0:T(8,128)S(1)}, s32[12,512]{1,0:T(8,128)}, u32[]{:S(2)}) copy-start(s32[12,512]{1,0:T(8,128)} %param.25) | copy-start | bytes 73732
  12.6 143.4 %copy-start.7 = (s32[12]{0:T(128)S(1)}, s32[12]{0:T(128)}, u32[]{:S(2)}) copy-start(s32[12]{0:T(128)} %param.27) | copy-start | bytes 148
  120.0 40.4 %copy-start.1 = (bf16[4096,256]{1,0:T(8,128)(2,1)S(1)}, bf16[4096,256]{1,0:T(8,128)(2,1)}, u32[]{:S(2)}) copy-start(bf16[4096,256]{1,0:T(8,128)(2,1)} %all-gather.3.cloned.1.call-done) | copy-start | bytes 6291460
  145.4 6.8 %collective-permute-start = (bf16[1,128,256]{1,2,0:T(8,128)(2,1)S(1)}, bf16[1,128,256]{1,2,0:T(8,128)(2,1)}, u32[]{:S(2)}, u32[]{:S(2)}) collective-permute-start(bf16[1,128,256]{1,2,0:T(8,128)(2,1)S(1)} %fusion.15), channel_id=1, source_target_pairs={{0,8},{8,16},{16,24},{24,32},{32,40},{40,48},{48,56},{56,64},{64,7... | collective-permute-start | bytes 196616 | tf_op jit(solution)/shard_map/ppermute | solution.py:14
  149.2 5.1 %collective-permute-start.1 = (bf16[1,128,256]{1,2,0:T(8,128)(2,1)S(1)}, bf16[1,128,256]{1,2,0:T(8,128)(2,1)}, u32[]{:S(2)}, u32[]{:S(2)}) collective-permute-start(bf16[1,128,256]{1,2,0:T(8,128)(2,1)S(1)} %fusion.15), channel_id=1, source_target_pairs={{8,0},{16,8},{24,16},{32,24},{40,32},{48,40},{56,48},{64,56},{72,6... | collective-permute-start | bytes 196616 | tf_op jit(solution)/shard_map/ppermute | solution.py:15
  160.4 73.2 %copy-start.4 = (pred[12,1536]{1,0:T(8,128)(4,1)S(1)}, pred[12,1536]{1,0:T(8,128)(4,1)}, u32[]{:S(2)}) copy-start(pred[12,1536]{1,0:T(8,128)(4,1)} %compare_and_fusion) | copy-start | bytes 55300
  233.6 10.2 %copy-start.3 = (s32[6144]{0:T(1024)S(1)}, s32[6144]{0:T(1024)}, u32[]{:S(2)}) copy-start(s32[6144]{0:T(1024)} %broadcast_clamp_fusion.1) | copy-start | bytes 73732
  281.2 194.7 %copy-start.6 = (pred[12,128]{1,0:T(8,128)(4,1)S(1)}, pred[12,128]{1,0:T(8,128)(4,1)}, u32[]{:S(2)}) copy-start(pred[12,128]{1,0:T(8,128)(4,1)} %broadcast_compare_fusion) | copy-start | bytes 4612
Sparse Core Ops, SparseCore 0:
  11.7 108.1 all-gather.2
  156.0 28.7 all-gather.4
where the time goes:
time: 486 us; the launch traced here: 484 us
  blocking collectives  171 us (35%)
  local copies, waits for them, and re-layouts  114 us (23%)
  waiting for transfers between devices  110 us (23%)
  matrix products  37.9 us (8%)
  other arithmetic  30.3 us (6%)
  between operations  14.9 us (3%)
  starting transfers between devices  5.17 us (1%)
    all_gather x12, blocking collectives, one_front(): lax.all_gather(partial_value, 'grid', axis=1, tiled=True)  159 us
    all_gather x1, waiting for transfers between devices, local(): lax.all_gather(top_solution, ('leaf', 'grid'), axis=0, tiled=True)  107 us
    gather x1, local copies, waits for them, and re-layouts, local(): from_top = jnp.take(ancestors, top_rows_two, axis=0)  73.2 us
    gather x1, local copies, waits for them, and re-layouts, local(): parent_rows = jnp.take(stacked, row_picks, axis=0)  25 us
    dot_general x13, matrix products, updated_rhs(): jnp.einsum('cus,cur->csr', factor, gathered, preferred_element_type=jnp.f...  22.9 us
    dot_general x13, matrix products, make_accumulate(): jnp.einsum('ckj,ckr->cjr', inverse, piece, preferred_element_type=jnp.flo...  15 us
    all_gather x1, blocking collectives, local(): lax.all_gather(partial_one, 'grid', axis=1, tiled=True)  12.6 us
    gather x1, local copies, waits for them, and re-layouts, local(): gathered_one = jnp.take(ancestors, top_rows_one, axis=0)  10.5 us
  transfers between devices with their start and end apart: 4, of which 2 were waited for; matrix products, arithmetic and copies ran while one was open for 19% of the time, Pallas kernels for 0%

commit v1 on v0

v1 whole, which is shorter than its diff:
```python
import functools

import jax
import jax.numpy as jnp
from jax import lax
from jax.experimental import pallas as pl
from jax.experimental.pallas import tpu as pltpu
from jax.sharding import PartitionSpec as P

MESH = pl.DeviceIdType.MESH
F32 = jnp.float32
BF = jnp.bfloat16

R = 256
B = 128
S = 1024
U = 2048
UT = 1536
UP = 512
C2 = 12
NX, NY, NZ = 4, 4, 8
LEAVES = NY * NZ
BS = 512
BD = 256

ONE = C2
LAG_B, LAG_C, LAG_D, LAG_E = 6, 8, 10, 12


def kernel(
    top, right1, upd1, inv1, rows1, right2, upd2, inv2, rows2, seps, parent_s, live1_s, live2_s,
    out1, out2,
    topb, topT, u1, i1, r1, t1, t1s, u2, i2, r2, t2, t2s, sp,
    acc, rbuf, s1, ob1, ob2,
    ld, ldsem_out,
    g_send, g_recv, a_send, a_recv, c_send, c_recv,
    x_send, x_recv, k_send, k_recv,
    nb_send, nb_recv, sx_send, sx_recv, sk_send, sk_recv,
):
    leaf = lax.axis_index("leaf")
    g = lax.axis_index("grid")
    z, y = leaf // NY, leaf % NY
    x, c = g // 2, g % 2
    sib = (leaf, x * 2 + (1 - c))

    def at_x(xx):
        return (leaf, xx * 2 + c)

    def rcopy(src, dst, ssem, rsem, dev):
        return pltpu.make_async_remote_copy(
            src_ref=src, dst_ref=dst, send_sem=ssem, recv_sem=rsem, device_id=dev, device_id_type=MESH
        )

    def same(ref, ssem, rsem, dev):
        return rcopy(ref, ref, ssem, rsem, dev)

    own_rows = topb.at[pl.ds(pl.multiple_of(g * 16, 16), 16), :]
    loads = [
        (top, own_rows),
        (upd1.at[0], u1),
        (rows1, t1s),
        (right1.at[0], r1),
        (inv1.at[0], i1),
        (rows2, t2s),
        (upd2, u2),
        (seps, sp),
        (right2, r2),
        (inv2, i2),
    ]
    loads += [(rows1.at[:, pl.ds(d * BD, BD)], t1.at[d]) for d in range(U // BD)]
    loads += [(rows2.at[:, pl.ds(d * BD, BD)], t2.at[d]) for d in range(UT // BD)]
    loads = [pltpu.make_async_copy(a, b, ld.at[i]) for i, (a, b) in enumerate(loads)]
    for copy in loads:
        copy.start()

    barrier = pltpu.get_barrier_semaphore()

    def greet(dev):
        pl.semaphore_signal(barrier, inc=1, device_id=dev, device_id_type=MESH)

    for d in range(1, 8):
        greet((leaf, (g + d) % 8))
    for d in range(1, NY):
        greet((z * NY + (y + d) % NY, g))
    for d in range(1, NZ):
        greet((((z + d) % NZ) * NY + y, g))

    @pl.when(leaf > 0)
    def _():
        greet((leaf - 1, g))

    @pl.when(leaf < LEAVES - 1)
    def _():
        greet((leaf + 1, g))

    for k in range(7):

        @pl.when(jnp.logical_and(k < g, jnp.logical_not(jnp.logical_and(g == 7, k == 5))))
        def _():
            def zero(f, carry):
                rbuf[f, k] = jnp.zeros((R, B), BF)
                return carry

            lax.fori_loop(0, C2 + 1, zero, 0)

    ends = jnp.where(leaf > 0, 1, 0) + jnp.where(leaf < LEAVES - 1, 1, 0)
    pl.semaphore_wait(barrier, 7 + (NY - 1) + (NZ - 1) + ends)

    loads[0].wait()
    for d in range(1, 8):
        rcopy(own_rows, own_rows, g_send.at[d - 1], g_recv.at[d - 1], (leaf, (g + d) % 8)).start()
    for d in range(1, 8):
        other = (g + 8 - d) % 8
        part = topb.at[pl.ds(pl.multiple_of(other * 16, 16), 16), :]
        same(part, g_send.at[d - 1], g_recv.at[d - 1], (leaf, other)).wait_recv()
    block = topb[...].astype(F32).T.astype(BF)
    topT[z, y] = block.reshape(2, 128, B)

    def yz(zz, yy):
        return (((zz + NZ) % NZ) * NY + (yy + NY) % NY, g)

    def hand(region, i):
        same(region, c_send.at[i], c_recv.at[i], sib).start()

    def pieces0():
        out = [topT.at[z, (y + NY - d) % NY, 0] for d in (1, 3, 2)]
        out += [topT.at[(z + NZ - k) % NZ, :, 0] for k in (1, 2, 3)] + [topT.at[(z + 4) % NZ, pl.ds(0, 2), 0]]
        out += [topT.at[(z + k) % NZ, :, 0] for k in (1, 2, 3)] + [topT.at[(z + 4) % NZ, pl.ds(2, 2), 0]]
        return out

    def pieces1():
        out = [topT.at[(z + NZ - i) % NZ, y, 1] for i in range(1, NZ)]
        out += [topT.at[:, (y + NY - 1) % NY, 1], topT.at[:, (y + 1) % NY, 1]]
        out += [topT.at[pl.ds(0, 4), (y + 2) % NY, 1], topT.at[pl.ds(4, 4), (y + 2) % NY, 1]]
        return out

    @pl.when(c == 0)
    def _():
        got = pieces0()

        def send(region, i, dev):
            same(region, a_send.at[i], a_recv.at[i], dev).start()

        def arrived(i):
            same(got[i], a_send.at[i], a_recv.at[i], sib).wait_recv()

        for i, d in enumerate((1, 3, 2)):
            send(topT.at[z, y, 0], i, yz(z, y + d))
        for i in range(3):
            arrived(i)
        for k in range(1, 5):
            right_src, left_src = topT.at[(z + NZ - k + 1) % NZ], topT.at[(z + k - 1) % NZ]
            if k < 4:
                send(right_src.at[:, 0], 2 + k, yz(z + 1, y))
                send(left_src.at[:, 0], 6 + k, yz(z - 1, y))
            else:
                send(right_src.at[pl.ds(0, 2), 0], 2 + k, yz(z + 1, y))
                send(left_src.at[pl.ds(2, 2), 0], 6 + k, yz(z - 1, y))
            if k == 1:
                for i in range(3):
                    hand(got[i], i)
            else:
                hand(got[1 + k], 1 + k)
                hand(got[5 + k], 5 + k)
            arrived(2 + k)
            arrived(6 + k)
        hand(got[6], 6)
        hand(got[10], 10)
        for i, region in enumerate(got):
            same(region, a_send.at[i], a_recv.at[i], sib).wait_send()
            same(region, c_send.at[i], c_recv.at[i], sib).wait_send()
        for i, region in enumerate(pieces1()):
            same(region, c_send.at[i], c_recv.at[i], sib).wait_recv()

    @pl.when(c == 1)
    def _():
        got = pieces1()

        def send(region, i, dev):
            same(region, a_send.at[i], a_recv.at[i], dev).start()

        def arrived(i):
            same(got[i], a_send.at[i], a_recv.at[i], sib).wait_recv()

        for i in (4, 3, 5, 2, 6, 1, 7):
            send(topT.at[z, y, 1], i - 1, yz(z + i, y))
        for i in range(7):
            arrived(i)
        send(topT.at[:, y, 1], 7, yz(z, y + 1))
        send(topT.at[:, y, 1], 8, yz(z, y - 1))
        for i in range(7):
            hand(got[i], i)
        arrived(7)
        send(topT.at[pl.ds(0, 4), (y + NY - 1) % NY, 1], 9, yz(z, y + 1))
        arrived(8)
        send(topT.at[pl.ds(4, 4), (y + 1) % NY, 1], 10, yz(z, y - 1))
        hand(got[7], 7)
        hand(got[8], 8)
        arrived(9)
        hand(got[9], 9)
        arrived(10)
        hand(got[10], 10)
        for i, region in enumerate(got):
            same(region, a_send.at[i], a_recv.at[i], sib).wait_send()
            same(region, c_send.at[i], c_recv.at[i], sib).wait_send()
        for i, region in enumerate(pieces0()):
            same(region, c_send.at[i], c_recv.at[i], sib).wait_recv()

    for copy in loads[1:]:
        copy.wait()

    def picked_product(count, front, vec, sca, factor):
        nd, ns = count // BD, (LEAVES * B) // BS
        total = jnp.zeros((R, B), F32)
        firsts = [sca[front, i * BD] for i in range(1, nd)]
        passed_at = []
        for i, v in enumerate(firsts):
            ends = jnp.int32(i)
            for j in range(1, ns):
                ends = ends + jnp.where(v >= j * BS, 1, 0)
            passed_at.append(ends)
        iota = lax.broadcasted_iota(jnp.int32, (BS, BD), 0)
        for t in range(nd + ns - 1):
            d = jnp.int32(0)
            for ends in passed_at:
                d = d + jnp.where(ends < t, 1, 0)
            s = t - d
            src = topT[s]
            lhs = jnp.concatenate([src[i].reshape(R, B) for i in range(BS // B)], axis=1)
            picks = vec[d, pl.ds(front, 1), :]
            onehot = jnp.where(iota == picks - s * BS, 1.0, 0.0).astype(BF)
            got = jnp.dot(lhs, onehot, preferred_element_type=F32).astype(BF)
            total = total + jnp.dot(got, factor(d), preferred_element_type=F32)
        return total

    def xs(f, i, k, dest):
        return same(rbuf.at[f, 2 * k + c], x_send.at[f, i], x_recv.at[f, k], at_x(dest))

    def ks(f, k, core):
        return same(rbuf.at[f, 2 * k + core], k_send.at[f, k], k_recv.at[f, k], sib)

    def x_arrived(f, k):
        xs(f, 0, k, 0).wait_recv()

    def own_sends(f, act):
        @pl.when(x == 3)
        def _():
            act(xs(f, 0, 3, 2))
            act(xs(f, 1, 3, 0))

        @pl.when(x == 2)
        def _():
            act(xs(f, 0, 2, 1))

            @pl.when(c == 1)
            def _():
                act(xs(f, 1, 2, 3))

        @pl.when(x == 1)
        def _():
            act(xs(f, 0, 1, 0))

        @pl.when(c == 1)
        def _():
            act(ks(f, x, c))

    def first_hop(f, wait, act):
        @pl.when(x == 0)
        def _():
            wait(f, 3)
            act(xs(f, 0, 3, 1))
            act(ks(f, 3, c))
            wait(f, 1)
            act(ks(f, 1, c))

        @pl.when(x == 1)
        def _():
            wait(f, 2)

            @pl.when(c == 0)
            def _():
                act(xs(f, 1, 2, 0))

            act(ks(f, 2, c))

        @pl.when(x == 2)
        def _():
            wait(f, 3)
            act(ks(f, 3, c))

        @pl.when(jnp.logical_and(x == 3, c == 1))
        def _():
            wait(f, 2)
            act(xs(f, 2, 2, 0))

    def second_hop(f, wait, act):
        @pl.when(x == 0)
        def _():
            wait(f, 2)
            act(ks(f, 2, c))

        @pl.when(x == 1)
        def _():
            wait(f, 3)
            act(ks(f, 3, c))

    def from_core(f):
        for k in range(4):

            @pl.when(jnp.logical_or(k > x, jnp.logical_and(k == x, c == 0)))
            def _():
                ks(f, k, 1 - c).wait_recv()

    def start(copy):
        copy.start()

    def drain(copy):
        copy.wait_send()

    def nothing(f, k):
        pass

    lanes = lax.broadcasted_iota(jnp.int32, (R, B), 1) + g * B

    def solve(f, inverse, live):
        lhs = jnp.concatenate([rbuf[f, k] for k in range(8)], axis=1)
        solved = jnp.dot(lhs, inverse, preferred_element_type=F32)
        return jnp.where(lanes < live, solved, 0.0)

    total1 = picked_product(U, 0, t1, t1s, lambda d: u1[d])
    rbuf[ONE, g] = (r1[...].astype(F32).T - total1).astype(BF)
    own_sends(ONE, start)

    def s1_x(slot, d):
        return same(s1.at[slot, g], sx_send.at[slot, d - 1], sx_recv.at[slot, d - 1], at_x((x + d) % NX))

    def s1_x_got(slot, d):
        return s1.at[slot, 2 * ((x + NX - d) % NX) + c]

    def s1_k(slot, k, core):
        return same(s1.at[slot, 2 * k + core], sk_send.at[slot, k], sk_recv.at[slot, k], sib)

    def with_slots(slots, body):
        for slot in slots:
            if slot == 1:
                body(slot)
            else:

                @pl.when((leaf > 0) if slot == 0 else (leaf < LEAVES - 1))
                def _():
                    body(slot)

    def s1_up():
        return rcopy(s1.at[1, g], s1.at[0, g], nb_send.at[0], nb_recv.at[0], (leaf + 1, g))

    def s1_down():
        return rcopy(s1.at[1, g], s1.at[2, g], nb_send.at[1], nb_recv.at[1], (leaf - 1, g))

    def solve_one():
        from_core(ONE)
        solved = solve(ONE, i1[...], live1_s[0])
        s1[1, g] = solved.astype(BF)

        @pl.when(leaf < LEAVES - 1)
        def _():
            s1_up().start()

        @pl.when(leaf > 0)
        def _():
            s1_down().start()

        spread(1)
        ob1[...] = solved.T.astype(BF)
        pltpu.make_async_copy(ob1, out1.at[0], ldsem_out.at[C2]).start()

    def spread(slot):
        for d in (2, 1, 3):
            s1_x(slot, d).start()
        s1_k(slot, x, c).start()

    def s1_neighbours():
        def body(slot):
            if slot == 0:
                s1_up().wait_recv()
            else:
                s1_down().wait_recv()
            spread(slot)

        with_slots((0, 2), body)

    def s1_cross(slots):
        def body(slot):
            for d in (1, 3, 2):
                same(s1_x_got(slot, d), sx_send.at[slot, d - 1], sx_recv.at[slot, d - 1], sib).wait_recv()
                s1_k(slot, (x + NX - d) % NX, c).start()

        with_slots(slots, body)

    def s1_end():
        def body(slot):
            for k in range(NX):
                s1_k(slot, k, 1 - c).wait_recv()

        with_slots((1, 0, 2), body)

    def top_part(f):
        acc[f] = picked_product(UT, f, t2, t2s, lambda d: u2[f, d])

    def parent_part(f):
        slot = jnp.clip(parent_s[f] - leaf + 1, 0, 2)
        block = s1[slot]
        lhs = jnp.concatenate([block[k] for k in range(8)], axis=1)
        total = acc[f]
        iota = lax.broadcasted_iota(jnp.int32, (S, BD), 0)
        for d in range(UP // BD):
            picks = sp[pl.ds(f, 1), pl.ds(d * BD, BD)]
            onehot = jnp.where(iota == picks, 1.0, 0.0).astype(BF)
            got = jnp.dot(lhs, onehot, preferred_element_type=F32).astype(BF)
            total = total + jnp.dot(got, u2[f, UT // BD + d], preferred_element_type=F32)
        rbuf[f, g] = (r2[f].astype(F32).T - total).astype(BF)
        own_sends(f, start)

    def solve_two(f):
        from_core(f)
        solved = solve(f, i2[f], live2_s[f])
        ob2[f] = solved.T.astype(BF)
        pltpu.make_async_copy(ob2.at[f], out2.at[f], ldsem_out.at[f]).start()

    def body(it, carry):
        pl.when(it == 1)(lambda: first_hop(ONE, x_arrived, start))
        pl.when(it == 2)(lambda: second_hop(ONE, x_arrived, start))
        pl.when(it == 3)(solve_one)

        @pl.when(it == 4)
        def _():
            s1_neighbours()
            s1_cross((1,))

        pl.when(it == 5)(lambda: s1_cross((0, 2)))
        pl.when(it == 6)(s1_end)

        def staged(lag, action):
            @pl.when(jnp.logical_and(it >= lag, it < C2 + lag))
            def _():
                action(it - lag)

        staged(LAG_C, lambda f: first_hop(f, x_arrived, start))
        staged(LAG_D, lambda f: second_hop(f, x_arrived, start))
        staged(LAG_B, parent_part)
        staged(LAG_E, solve_two)
        staged(0, top_part)
        return carry

    lax.fori_loop(0, C2 + LAG_E, body, 0)

    for d in range(1, 8):
        rcopy(own_rows, own_rows, g_send.at[d - 1], g_recv.at[d - 1], (leaf, (g + d) % 8)).wait_send()

    def finish(f, carry):
        own_sends(f, drain)
        first_hop(f, nothing, drain)
        second_hop(f, nothing, drain)
        return carry

    lax.fori_loop(0, C2 + 1, finish, 0)

    def finish_slot(slot):
        for d in range(1, 4):
            s1_x(slot, d).wait_send()
        for k in range(NX):
            s1_k(slot, k, c).wait_send()

    with_slots((0, 1, 2), finish_slot)

    @pl.when(leaf < LEAVES - 1)
    def _():
        s1_up().wait_send()

    @pl.when(leaf > 0)
    def _():
        s1_down().wait_send()

    pltpu.make_async_copy(ob1, out1.at[0], ldsem_out.at[C2]).wait()

    def finish_out(f, carry):
        pltpu.make_async_copy(ob2.at[f], out2.at[f], ldsem_out.at[f]).wait()
        return carry

    lax.fori_loop(0, C2, finish_out, 0)


def local(
    top_solution, right_one, update_one, inverse_one, top_rows_one, live_one,
    right_two, update_two, inverse_two, top_rows_two, sep_rows, parent, live_two,
):
    anywhere = pl.BlockSpec(memory_space=pl.ANY)
    scalar = pl.BlockSpec(memory_space=pltpu.SMEM)
    dma = pltpu.SemaphoreType.DMA
    vm = pltpu.VMEM
    return pl.pallas_call(
        kernel,
        out_shape=(
            jax.ShapeDtypeStruct((1, B, R), BF),
            jax.ShapeDtypeStruct((C2, B, R), BF),
        ),
        in_specs=[anywhere] * 10 + [scalar] * 3,
        out_specs=(anywhere, anywhere),
        scratch_shapes=[
            vm((B, R), BF),
            vm((NZ, NY, 2, 128, B), BF),
            vm((U // BD, BD, B), BF),
            vm((S, B), BF),
            vm((B, R), BF),
            vm((U // BD, 1, BD), jnp.int32),
            pltpu.SMEM((1, U), jnp.int32),
            vm((C2, U // BD, BD, B), BF),
            vm((C2, S, B), BF),
            vm((C2, B, R), BF),
            vm((UT // BD, C2, BD), jnp.int32),
            pltpu.SMEM((C2, UT), jnp.int32),
            vm((C2, UP), jnp.int32),
            vm((C2, R, B), F32),
            vm((C2 + 1, 8, R, B), BF),
            vm((3, 8, R, B), BF),
            vm((B, R), BF),
            vm((C2, B, R), BF),
            dma((24,)), dma((C2 + 1,)),
            dma((7,)), dma((7,)), dma((11,)), dma((11,)), dma((11,)), dma((11,)),
            dma((C2 + 1, 3)), dma((C2 + 1, 4)), dma((C2 + 1, 4)), dma((C2 + 1, 4)),
            dma((2,)), dma((2,)), dma((3, 3)), dma((3, 3)), dma((3, 4)), dma((3, 4)),
        ],
        compiler_params=pltpu.CompilerParams(
            collective_id=0, has_side_effects=True, vmem_limit_bytes=56 * 1024 * 1024
        ),
        cost_estimate=pl.CostEstimate(flops=20_000_000_000, bytes_accessed=12_000_000, transcendentals=0),
        name="adjoint_solve",
    )(
        top_solution, right_one, update_one.reshape(1, U // BD, BD, B), inverse_one, top_rows_one,
        right_two, update_two.reshape(C2, U // BD, BD, B), inverse_two, top_rows_two, sep_rows,
        parent, live_one, live_two,
    )


def solution(mesh):
    in_specs = (
        P(("leaf", "grid"), None),
        P("leaf", "grid", None),
        P("leaf", None, "grid"),
        P("leaf", None, "grid"),
        P("leaf", None),
        P("leaf"),
        P("leaf", "grid", None),
        P("leaf", None, "grid"),
        P("leaf", None, "grid"),
        P("leaf", None),
        P("leaf", None),
        P("leaf"),
        P("leaf"),
    )
    out_specs = (P("leaf", "grid", None), P("leaf", "grid", None))
    return jax.shard_map(local, mesh=mesh, in_specs=in_specs, out_specs=out_specs, check_vma=False)
```

time: 486 us -> 120 us (0.25)
  blocking collectives: 171 us -> 0 us
  Pallas kernels: 0 us -> 113 us
  local copies, waits for them, and re-layouts: 114 us -> 3.54 us
  waiting for transfers between devices: 110 us -> 0 us
  matrix products: 37.9 us -> 0 us
  other arithmetic: 30.3 us -> 0 us
  between operations: 14.9 us -> 1.29 us
  starting transfers between devices: 5.17 us -> 0 us
    all_gather x13 -> x0, blocking collectives: 171 us -> none  [the longest x12 159 us: one_front(): lax.all_gather(partial_value, 'grid', axis=1, tiled=True)]
    pallas_call x0 -> x1, Pallas kernels: none -> 113 us  [local(): pl.pallas_call(kernel, out_shape=(jax.ShapeDtypeStruct((1, B, R), BF), ja...]
    gather x3 -> x0, local copies, waits for them, and re-layouts: 109 us -> none  [the longest x1 73.2 us: local(): from_top = jnp.take(ancestors, top_rows_two, axis=0)]
    all_gather x2 -> x0, waiting for transfers between devices: 107 us -> none  [the longest x1 107 us: local(): lax.all_gather(top_solution, ('leaf', 'grid'), axis=0, tiled=True)]
    dot_general x26 -> x0, matrix products: 37.9 us -> none  [the longest x13 22.9 us: updated_rhs(): jnp.einsum('cus,cur->csr', factor, gathered, preferred_element_type=jnp.f...]
    select_n x3 -> x0, other arithmetic: 13.2 us -> none  [the longest x2 9.99 us: local(): from_top = jnp.take(ancestors, top_rows_two, axis=0)]
    concatenate x2 -> x0, other arithmetic: 10.8 us -> none  [the longest x1 9.25 us: local(): gathered_two = jnp.concatenate([from_top, parent_rows], axis=1)]
    ppermute x2 -> x0, starting transfers between devices: 5.1 us -> none  [the longest x1 3.82 us: with_halo(): before = lax.ppermute(last, axis, up)]
  transfers between devices with their start and end apart: 4 -> 0, of which waited for: 2 -> 0; matrix products, arithmetic and copies ran while one was open for 19% -> 0% of each run, Pallas kernels for 0% -> 0%
where the time goes in v1:
time: 120 us; the launch traced here: 118 us
  Pallas kernels  113 us (94%)
  local copies, waits for them, and re-layouts  3.54 us (3%)
  between operations  1.29 us (1%)
    pallas_call x1, Pallas kernels, local(): pl.pallas_call(kernel, out_shape=(jax.ShapeDtypeStruct((1, B, R), BF), ja...  113 us
    unnamed x2, local copies, waits for them, and re-layouts  3.54 us

profile of v1, /device:TPU:1, one launch (start us, length us, event | category | flops | bytes accessed | tf_op | source)
XLA Modules:
  0.0 117.6 jit_solution(17213502575999647746)
XLA Ops:
  1.3 112.8 %adjoint_solve.1 = (bf16[1,128,256]{2,1,0:T(8,128)(2,1)}, bf16[12,128,256]{2,1,0:T(8,128)(2,1)}) custom-call(bf16[16,256]{1,0:T(8,128)(2,1)} %top.1, bf16[1,128,256]{2,1,0:T(8,128)(2,1)} %right1.1, bf16[1,8,256,128]{3,2,1,0:T(8,128)(2,1)} %bitcast.3, bf16[1,1024,128]{2,1,0:T(8,128)(2,1)} %inv1.1, s32[1,2048]{1,0:T(1,128)} %rows1.1, ...), custom_call_target="tpu_custom_call" | custom-call | flops 20000000000 | bytes 12000000 | tf_op jit(solution)/shard_map/adjoint_solve/pallas_call | solution.py:500
  114.1 1.5 %copy.18 = bf16[1,128,256]{2,1,0:T(8,128)(2,1)} copy(bf16[1,128,256]{2,1,0:T(8,128)(2,1)} %get-tuple-element.4) | data formatting | bytes 131072
  115.6 2.1 %copy.19 = bf16[12,128,256]{2,1,0:T(8,128)(2,1)} copy(bf16[12,128,256]{2,1,0:T(8,128)(2,1)} %get-tuple-element.5) | data formatting | bytes 1572864

commit v2 on v1

v2 whole, which is shorter than its diff:
```python
import functools

import jax
import jax.numpy as jnp
from jax import lax
from jax.experimental import pallas as pl
from jax.experimental.pallas import tpu as pltpu
from jax.sharding import PartitionSpec as P

MESH = pl.DeviceIdType.MESH
F32 = jnp.float32
BF = jnp.bfloat16

R = 256
B = 128
S = 1024
U = 2048
UT = 1536
UP = 512
C2 = 12
NX, NY, NZ = 4, 4, 8
LEAVES = NY * NZ
BS = 256
DELAY = 3
BD = 256

ONE = C2
H = S // 2
LAG_B, LAG_C, LAG_D, LAG_E = 6, 10, 11, 14


def kernel(
    top, right1, upd1, inv1, rows1, right2, upd2, inv2, rows2, seps, parent_s, live1_s, live2_s,
    out1, out2,
    topb, topT, u1, r1, t1, t1s, u2, r2, t2, t2s, sp, sps, iv,
    acc, rbuf, pbuf, pout, s1, ob1, ob2,
    ld, ldsem_out,
    g_send, g_recv, a_send, a_recv, c_send, c_recv,
    i_send, i_recv, x_send, x_recv, k_send, k_recv, p_send, p_recv,
    nb_send, nb_recv, sx_send, sx_recv, sk_send, sk_recv,
):
    leaf = lax.axis_index("leaf")
    g = lax.axis_index("grid")
    z, y = leaf // NY, leaf % NY
    x, c = g // 2, g % 2
    sib = (leaf, x * 2 + (1 - c))

    def at_x(xx):
        return (leaf, xx * 2 + c)

    def rcopy(src, dst, ssem, rsem, dev):
        return pltpu.make_async_remote_copy(
            src_ref=src, dst_ref=dst, send_sem=ssem, recv_sem=rsem, device_id=dev, device_id_type=MESH
        )

    def same(ref, ssem, rsem, dev):
        return rcopy(ref, ref, ssem, rsem, dev)

    own_rows = topb.at[pl.ds(pl.multiple_of(g * 16, 16), 16), :]
    half = pl.ds(pl.multiple_of(jnp.where(x >= 2, H, 0), H), H)
    loads = [
        (top, own_rows),
        (upd1.at[0], u1),
        (rows1, t1s),
        (right1.at[0], r1),
        (inv1.at[0, half], iv.at[ONE, :, pl.ds(0, B)]),
        (rows2, t2s),
        (upd2, u2),
        (seps, sps),
        (right2, r2),
        (inv2.at[:, half], iv.at[pl.ds(0, C2), :, pl.ds(0, B)]),
    ]
    loads += [(rows1.at[:, pl.ds(d * BD, BD)], t1.at[d]) for d in range(U // BD)]
    loads += [(rows2.at[:, pl.ds(d * BD, BD)], t2.at[d]) for d in range(UT // BD)]
    loads += [(seps.at[:, pl.ds(d * BD, BD)], sp.at[d]) for d in range(UP // BD)]
    loads = [pltpu.make_async_copy(a, b, ld.at[i]) for i, (a, b) in enumerate(loads)]
    for copy in loads:
        copy.start()

    barrier = pltpu.get_barrier_semaphore()

    def greet(dev):
        pl.semaphore_signal(barrier, inc=1, device_id=dev, device_id_type=MESH)

    for d in range(1, 8):
        greet((leaf, (g + d) % 8))
    for d in range(1, NY):
        greet((z * NY + (y + d) % NY, g))
    for d in range(1, NZ):
        greet((((z + d) % NZ) * NY + y, g))

    @pl.when(leaf > 0)
    def _():
        greet((leaf - 1, g))

    @pl.when(leaf < LEAVES - 1)
    def _():
        greet((leaf + 1, g))

    @pl.when(x == 1)
    def _():
        def zero(f, carry):
            for k in range(2):
                rbuf[f, k] = jnp.zeros((R, B), BF)
            return carry

        lax.fori_loop(0, C2 + 1, zero, 0)

    ends = jnp.where(leaf > 0, 1, 0) + jnp.where(leaf < LEAVES - 1, 1, 0)
    pl.semaphore_wait(barrier, 7 + (NY - 1) + (NZ - 1) + ends)

    loads[0].wait()
    for d in range(1, 8):
        rcopy(own_rows, own_rows, g_send.at[d - 1], g_recv.at[d - 1], (leaf, (g + d) % 8)).start()
    def ship(f):
        src = inv1.at[0, pl.ds(H, H)] if f is ONE else inv2.at[f, pl.ds(H, H)]
        return rcopy(src, iv.at[f, :, pl.ds(B, B)], i_send.at[f], i_recv.at[f], at_x(3 - x))

    def each_front(action):
        def one(f, carry):
            action(f)
            return carry

        lax.fori_loop(0, C2, one, 0)

    @pl.when(x < 2)
    def _():
        ship(ONE).start()
        each_front(lambda f: ship(f).start())

    for d in range(1, 8):
        other = (g + 8 - d) % 8
        part = topb.at[pl.ds(pl.multiple_of(other * 16, 16), 16), :]
        same(part, g_send.at[d - 1], g_recv.at[d - 1], (leaf, other)).wait_recv()
    block = topb[...].astype(F32).T.astype(BF)
    topT[z, y // 2, y % 2] = block.reshape(2, 128, B)

    def yz(zz, yy):
        return (((zz + NZ) % NZ) * NY + (yy + NY) % NY, g)

    def hand(region, i):
        same(region, c_send.at[i], c_recv.at[i], sib).start()

    def block_at(zz, yy, core):
        zz, yy = (zz + NZ) % NZ, (yy + NY) % NY
        return topT.at[zz, yy // 2, yy % 2, core]

    def plane(zz):
        return topT.at[(zz + NZ) % NZ, :, :, 0]

    def half_plane(zz, i):
        return topT.at[(zz + NZ) % NZ, i, :, 0]

    def column(yy):
        yy = (yy + NY) % NY
        return topT.at[:, yy // 2, yy % 2, 1]

    def pieces0():
        out = [block_at(z, y - d, 0) for d in (1, 3, 2)]
        out += [plane(z - 1), plane(z + 1), plane(z - 2), plane(z + 2)]
        return out + [plane(z - 3), plane(z + 3), half_plane(z - 4, 0), half_plane(z + 4, 1)]

    def pieces1():
        return [block_at(z - i, y, 1) for i in range(1, NZ)] + [column(y - d) for d in (1, 3, 2)]

    def send(region, i, dev):
        same(region, a_send.at[i], a_recv.at[i], dev).start()

    def gone(got, other):
        for i, region in enumerate(got):
            same(region, a_send.at[i], a_recv.at[i], sib).wait_send()
            same(region, c_send.at[i], c_recv.at[i], sib).wait_send()
        for i, region in enumerate(other):
            same(region, c_send.at[i], c_recv.at[i], sib).wait_recv()

    @pl.when(c == 0)
    def _():
        got = pieces0()

        def arrived(i):
            same(got[i], a_send.at[i], a_recv.at[i], sib).wait_recv()

        for i, d in enumerate((1, 3, 2)):
            send(block_at(z, y, 0), i, yz(z, y + d))
        for i in range(3):
            arrived(i)
        for i, d in ((5, 2), (6, -2), (3, 1), (4, -1)):
            send(plane(z), i, yz(z + d, y))
        for i in range(3):
            hand(got[i], i)
        for i in (3, 4):
            arrived(i)
            hand(got[i], i)
        arrived(5)
        send(plane(z - 2), 7, yz(z + 1, y))
        send(half_plane(z - 2, 0), 9, yz(z + 2, y))
        arrived(6)
        send(plane(z + 2), 8, yz(z - 1, y))
        send(half_plane(z + 2, 1), 10, yz(z - 2, y))
        for i in (5, 6):
            hand(got[i], i)
        for i in (7, 8, 9, 10):
            arrived(i)
            hand(got[i], i)
        gone(got, pieces1())

    @pl.when(c == 1)
    def _():
        got = pieces1()

        def arrived(i):
            same(got[i], a_send.at[i], a_recv.at[i], sib).wait_recv()

        for i in (4, 3, 5, 2, 6, 1, 7):
            send(block_at(z, y, 1), i - 1, yz(z + i, y))
        for i in range(7):
            arrived(i)
        for i, d in ((9, 2), (7, 1), (8, 3)):
            send(column(y), i, yz(z, y + d))
        for i in range(7):
            hand(got[i], i)
        for i in (7, 8, 9):
            arrived(i)
            hand(got[i], i)
        gone(got, pieces0())

    for copy in loads[1:]:
        copy.wait()

    def picked_product(count, pool, front, vec, sca, source, factor):
        nd, ns = count // BD, pool // BS
        total = jnp.zeros((R, B), F32)
        firsts = [sca[front, i * BD] for i in range(1, nd)]
        passed_at = []
        for i, v in enumerate(firsts):
            ends = jnp.int32(i)
            for j in range(1, ns):
                ends = ends + jnp.where(v >= j * BS, 1, 0)
            passed_at.append(ends)
        iota = lax.broadcasted_iota(jnp.int32, (BS, BD), 0)
        steps = nd + ns - 1
        pending = []
        for t in range(steps):
            d = jnp.int32(0)
            for ends in passed_at:
                d = d + jnp.where(ends < t, 1, 0)
            s = t - d
            picks = vec[d, pl.ds(front, 1), :]
            onehot = jnp.where(iota == picks - s * BS, 1.0, 0.0).astype(BF)
            got = jnp.dot(source(s), onehot, preferred_element_type=F32).astype(BF)
            pending.append((got, d))
            while len(pending) > (DELAY if t < steps - 1 else 0):
                got, d = pending.pop(0)
                total = total + jnp.dot(got, factor(d), preferred_element_type=F32)
        return total

    def top_rows(s):
        pair = topT[s >> 1, s & 1]
        return jnp.concatenate([pair[i].reshape(R, B) for i in range(2)], axis=1)

    twin = jnp.where(x >= 2, 5 - x, jnp.where(x == 1, 0, 1))
    sends, gets = x >= 1, x != 1

    def xs(f, k, dest):
        return same(rbuf.at[f, 2 * k + c], x_send.at[f], x_recv.at[f], at_x(dest))

    def ks(f, i, k, core):
        return same(rbuf.at[f, 2 * k + core], k_send.at[f, i], k_recv.at[f, i], sib)

    def ps(f):
        return rcopy(pout.at[f], pbuf.at[f], p_send.at[f], p_recv.at[f], at_x(3 - x))

    def own_sends(f):
        @pl.when(sends)
        def _():
            xs(f, x, twin).start()

        ks(f, 0, x, c).start()

    def first_hop(f):
        @pl.when(gets)
        def _():
            xs(f, twin, twin).wait_recv()
            ks(f, 1, twin, c).start()

    def from_core(f):
        ks(f, 0, x, 1 - c).wait_recv()

        @pl.when(gets)
        def _():
            ks(f, 1, twin, 1 - c).wait_recv()

    lanes = lax.broadcasted_iota(jnp.int32, (R, B), 1) + g * B

    def upper(f, live, out):
        from_core(f)
        if f is ONE:
            ship(ONE).wait_recv()
        else:
            ship(f).wait_recv()
        lhs = jnp.concatenate([rbuf[f, 4 + k] for k in range(4)], axis=1)
        both = jnp.dot(lhs, iv[f], preferred_element_type=F32)
        pout[f] = both[:, B:].astype(BF)
        ps(f).start()
        out(jnp.where(lanes < live, both[:, :B], 0.0))

    def lower(f, live, out):
        from_core(f)
        lhs = jnp.concatenate([rbuf[f, k] for k in range(4)], axis=1)
        own = jnp.dot(lhs, iv[f, :, :B], preferred_element_type=F32)
        ps(f).wait_recv()
        out(jnp.where(lanes < live, own + pbuf[f].astype(F32), 0.0))

    total1 = picked_product(U, LEAVES * B, 0, t1, t1s, top_rows, lambda d: u1[d])
    rbuf[ONE, g] = (r1[...].astype(F32).T - total1).astype(BF)
    own_sends(ONE)

    def s1_x(slot, d):
        return same(s1.at[slot, g], sx_send.at[slot, d - 1], sx_recv.at[slot, d - 1], at_x((x + d) % NX))

    def s1_x_got(slot, d):
        return s1.at[slot, 2 * ((x + NX - d) % NX) + c]

    def s1_k(slot, k, core):
        return same(s1.at[slot, 2 * k + core], sk_send.at[slot, k], sk_recv.at[slot, k], sib)

    def with_slots(slots, body):
        for slot in slots:
            if slot == 1:
                body(slot)
            else:

                @pl.when((leaf > 0) if slot == 0 else (leaf < LEAVES - 1))
                def _():
                    body(slot)

    def s1_up():
        return rcopy(s1.at[1, g], s1.at[0, g], nb_send.at[0], nb_recv.at[0], (leaf + 1, g))

    def s1_down():
        return rcopy(s1.at[1, g], s1.at[2, g], nb_send.at[1], nb_recv.at[1], (leaf - 1, g))

    def out_one(solved):
        s1[1, g] = solved.astype(BF)

        @pl.when(leaf < LEAVES - 1)
        def _():
            s1_up().start()

        @pl.when(leaf > 0)
        def _():
            s1_down().start()

        spread(1)
        ob1[...] = solved.T.astype(BF)
        pltpu.make_async_copy(ob1, out1.at[0], ldsem_out.at[C2]).start()

    def spread(slot):
        def over_x():
            for d in (2, 1, 3):
                s1_x(slot, d).start()

        if slot == 1:
            over_x()
        else:
            pl.when(c == 0)(over_x)
        s1_k(slot, x, c).start()

    def s1_relay(d, act):
        k = 2 * ((x + NX - d) % NX) + c

        @pl.when(leaf < LEAVES - 1)
        def _():
            act(rcopy(s1.at[1, k], s1.at[0, k], sx_send.at[0, d - 1], sx_recv.at[0, d - 1], (leaf + 1, g)))

        @pl.when(leaf > 0)
        def _():
            act(rcopy(s1.at[1, k], s1.at[2, k], sx_send.at[2, d - 1], sx_recv.at[2, d - 1], (leaf - 1, g)))

    def s1_neighbours():
        def body(slot):
            if slot == 0:
                s1_up().wait_recv()
            else:
                s1_down().wait_recv()
            spread(slot)

        with_slots((0, 2), body)

    def s1_cross(slots):
        def body(slot):
            for d in (1, 3, 2):
                same(s1_x_got(slot, d), sx_send.at[slot, d - 1], sx_recv.at[slot, d - 1], sib).wait_recv()
                if slot == 1:
                    pl.when(c == 1)(lambda: s1_relay(d, lambda copy: copy.start()))
                s1_k(slot, (x + NX - d) % NX, c).start()

        with_slots(slots, body)

    def s1_end():
        def body(slot):
            for k in range(NX):
                s1_k(slot, k, 1 - c).wait_recv()

        with_slots((1, 0, 2), body)

    def top_part(f):
        acc[f] = picked_product(UT, LEAVES * B, f, t2, t2s, top_rows, lambda d: u2[f, d])

    def parent_part(f):
        slot = jnp.clip(parent_s[f] - leaf + 1, 0, 2)

        def parent_rows(s):
            return jnp.concatenate([s1[slot, 2 * s], s1[slot, 2 * s + 1]], axis=1)

        total = picked_product(UP, S, f, sp, sps, parent_rows, lambda d: u2[f, UT // BD + d])
        rbuf[f, g] = (r2[f].astype(F32).T - acc[f] - total).astype(BF)
        own_sends(f)

    def out_two(f):
        def out(solved):
            ob2[f] = solved.T.astype(BF)
            pltpu.make_async_copy(ob2.at[f], out2.at[f], ldsem_out.at[f]).start()

        return out

    def body(it, carry):
        pl.when(it == 1)(lambda: first_hop(ONE))
        pl.when(jnp.logical_and(it == 2, x >= 2))(lambda: upper(ONE, live1_s[0], out_one))
        pl.when(jnp.logical_and(it == 3, x < 2))(lambda: lower(ONE, live1_s[0], out_one))

        @pl.when(jnp.logical_and(it == 4, c == 0))
        def _():
            s1_neighbours()
            s1_cross((1,))

        @pl.when(jnp.logical_and(it == 4, c == 1))
        def _():
            s1_cross((1,))
            s1_neighbours()

        pl.when(it == 5)(lambda: s1_cross((0, 2)))
        pl.when(it == 6)(s1_end)

        def staged(lag, action):
            @pl.when(jnp.logical_and(it >= lag, it < C2 + lag))
            def _():
                action(it - lag)

        def two_upper(f):
            pl.when(x >= 2)(lambda: upper(f, live2_s[f], out_two(f)))

        def two_lower(f):
            pl.when(x < 2)(lambda: lower(f, live2_s[f], out_two(f)))

        staged(LAG_C, first_hop)
        staged(LAG_D, two_upper)
        staged(LAG_B, parent_part)
        staged(LAG_E, two_lower)
        @pl.when(it < C2 // 2)
        def _():
            top_part(2 * it)
            top_part(2 * it + 1)

        return carry

    lax.fori_loop(0, C2 + LAG_E, body, 0)

    for d in range(1, 8):
        rcopy(own_rows, own_rows, g_send.at[d - 1], g_recv.at[d - 1], (leaf, (g + d) % 8)).wait_send()

    def finish(f, carry):
        ks(f, 0, x, c).wait_send()

        @pl.when(sends)
        def _():
            xs(f, x, twin).wait_send()

        @pl.when(gets)
        def _():
            ks(f, 1, twin, c).wait_send()

        @pl.when(x >= 2)
        def _():
            ps(f).wait_send()

        return carry

    lax.fori_loop(0, C2 + 1, finish, 0)

    @pl.when(x < 2)
    def _():
        ship(ONE).wait_send()
        each_front(lambda f: ship(f).wait_send())

    def finish_slot(slot):
        def over_x():
            for d in range(1, 4):
                s1_x(slot, d).wait_send()

        if slot == 1:
            over_x()
        else:
            pl.when(c == 0)(over_x)
        for k in range(NX):
            s1_k(slot, k, c).wait_send()

    @pl.when(c == 1)
    def _():
        for d in range(1, 4):
            s1_relay(d, lambda copy: copy.wait_send())

    with_slots((0, 1, 2), finish_slot)

    @pl.when(leaf < LEAVES - 1)
    def _():
        s1_up().wait_send()

    @pl.when(leaf > 0)
    def _():
        s1_down().wait_send()

    pltpu.make_async_copy(ob1, out1.at[0], ldsem_out.at[C2]).wait()

    def finish_out(f, carry):
        pltpu.make_async_copy(ob2.at[f], out2.at[f], ldsem_out.at[f]).wait()
        return carry

    lax.fori_loop(0, C2, finish_out, 0)


def local(
    top_solution, right_one, update_one, inverse_one, top_rows_one, live_one,
    right_two, update_two, inverse_two, top_rows_two, sep_rows, parent, live_two,
):
    anywhere = pl.BlockSpec(memory_space=pl.ANY)
    scalar = pl.BlockSpec(memory_space=pltpu.SMEM)
    dma = pltpu.SemaphoreType.DMA
    vm = pltpu.VMEM
    return pl.pallas_call(
        kernel,
        out_shape=(
            jax.ShapeDtypeStruct((1, B, R), BF),
            jax.ShapeDtypeStruct((C2, B, R), BF),
        ),
        in_specs=[anywhere] * 10 + [scalar] * 3,
        out_specs=(anywhere, anywhere),
        scratch_shapes=[
            vm((B, R), BF),
            vm((NZ, 2, 2, 2, 128, B), BF),
            vm((U // BD, BD, B), BF),
            vm((B, R), BF),
            vm((U // BD, 1, BD), jnp.int32),
            pltpu.SMEM((1, U), jnp.int32),
            vm((C2, U // BD, BD, B), BF),
            vm((C2, B, R), BF),
            vm((UT // BD, C2, BD), jnp.int32),
            pltpu.SMEM((C2, UT), jnp.int32),
            vm((UP // BD, C2, BD), jnp.int32),
            pltpu.SMEM((C2, UP), jnp.int32),
            vm((C2 + 1, H, 2 * B), BF),
            vm((C2, R, B), F32),
            vm((C2 + 1, 8, R, B), BF),
            vm((C2 + 1, R, B), BF),
            vm((C2 + 1, R, B), BF),
            vm((3, 8, R, B), BF),
            vm((B, R), BF),
            vm((C2, B, R), BF),
            dma((26,)), dma((C2 + 1,)),
            dma((7,)), dma((7,)), dma((11,)), dma((11,)), dma((11,)), dma((11,)),
            dma((C2 + 1,)), dma((C2 + 1,)), dma((C2 + 1,)), dma((C2 + 1,)), dma((C2 + 1, 2)), dma((C2 + 1, 2)),
            dma((C2 + 1,)), dma((C2 + 1,)),
            dma((2,)), dma((2,)), dma((3, 3)), dma((3, 3)), dma((3, 4)), dma((3, 4)),
        ],
        compiler_params=pltpu.CompilerParams(
            collective_id=0, has_side_effects=True, vmem_limit_bytes=56 * 1024 * 1024
        ),
        cost_estimate=pl.CostEstimate(flops=20_000_000_000, bytes_accessed=12_000_000, transcendentals=0),
        name="adjoint_solve",
    )(
        top_solution, right_one, update_one.reshape(1, U // BD, BD, B), inverse_one, top_rows_one,
        right_two, update_two.reshape(C2, U // BD, BD, B), inverse_two, top_rows_two, sep_rows,
        parent, live_one, live_two,
    )


def solution(mesh):
    in_specs = (
        P(("leaf", "grid"), None),
        P("leaf", "grid", None),
        P("leaf", None, "grid"),
        P("leaf", None, "grid"),
        P("leaf", None),
        P("leaf"),
        P("leaf", "grid", None),
        P("leaf", None, "grid"),
        P("leaf", None, "grid"),
        P("leaf", None),
        P("leaf", None),
        P("leaf"),
        P("leaf"),
    )
    out_specs = (P("leaf", "grid", None), P("leaf", "grid", None))
    return jax.shard_map(local, mesh=mesh, in_specs=in_specs, out_specs=out_specs, check_vma=False)
```

time: 120 us -> 91.7 us (0.76); the launches traced: 118 us -> 91.3 us
  Pallas kernels: 113 us -> 86.5 us
    pallas_call x1, Pallas kernels: 113 us -> 86.5 us  [local(): pl.pallas_call(kernel, out_shape=(jax.ShapeDtypeStruct((1, B, R), BF), ja...]
where the time goes in v2:
time: 91.7 us; the launch traced here: 91.3 us
  Pallas kernels  86.5 us (94%)
  local copies, waits for them, and re-layouts  3.54 us (4%)
  between operations  1.29 us (1%)
    pallas_call x1, Pallas kernels, local(): pl.pallas_call(kernel, out_shape=(jax.ShapeDtypeStruct((1, B, R), BF), ja...  86.5 us
    unnamed x2, local copies, waits for them, and re-layouts  3.54 us

profile of v2, /device:TPU:1, one launch (start us, length us, event | category | flops | bytes accessed | tf_op | source)
XLA Modules:
  0.0 91.3 jit_solution(16659386872350368239)
XLA Ops:
  1.3 86.5 %adjoint_solve.1 = (bf16[1,128,256]{2,1,0:T(8,128)(2,1)}, bf16[12,128,256]{2,1,0:T(8,128)(2,1)}) custom-call(bf16[16,256]{1,0:T(8,128)(2,1)} %top.1, bf16[1,128,256]{2,1,0:T(8,128)(2,1)} %right1.1, bf16[1,8,256,128]{3,2,1,0:T(8,128)(2,1)} %bitcast.3, bf16[1,1024,128]{2,1,0:T(8,128)(2,1)} %inv1.1, s32[1,2048]{1,0:T(1,128)} %rows1.1, ...), custom_call_target="tpu_custom_call" | custom-call | flops 20000000000 | bytes 12000000 | tf_op jit(solution)/shard_map/adjoint_solve/pallas_call | solution.py:540
  87.7 1.5 %copy.18 = bf16[1,128,256]{2,1,0:T(8,128)(2,1)} copy(bf16[1,128,256]{2,1,0:T(8,128)(2,1)} %get-tuple-element.4) | data formatting | bytes 131072
  89.2 2.1 %copy.19 = bf16[12,128,256]{2,1,0:T(8,128)(2,1)} copy(bf16[12,128,256]{2,1,0:T(8,128)(2,1)} %get-tuple-element.5) | data formatting | bytes 1572864

commit v3 on v2

--- a/solution.py
+++ b/solution.py
@@ -26,17 +26,18 @@
 
 ONE = C2
 H = S // 2
-LAG_B, LAG_C, LAG_D, LAG_E = 6, 10, 11, 14
+LAG_B, LAG_C, LAG_D, LAG_E = 11, 15, 16, 19
 
 
 def kernel(
-    top, right1, upd1, inv1, rows1, right2, upd2, inv2, rows2, seps, parent_s, live1_s, live2_s,
+    top, right1, upd1, inv1, rows1, right2, upd2, inv2, rows2, seps, live1, parent_s, live2_s,
     out1, out2,
-    topb, topT, u1, r1, t1, t1s, u2, r2, t2, t2s, sp, sps, iv,
+    topb, topT, u1, r1, t1, t1s, u2, r2, t2, t2s, sp, sps, iv, i1, live1_s,
     acc, rbuf, pbuf, pout, s1, ob1, ob2,
     ld, ldsem_out,
     g_send, g_recv, a_send, a_recv, c_send, c_recv,
     i_send, i_recv, x_send, x_recv, k_send, k_recv, p_send, p_recv,
+    o_send, o_recv, ok_send, ok_recv,
     nb_send, nb_recv, sx_send, sx_recv, sk_send, sk_recv,
 ):
     leaf = lax.axis_index("leaf")
@@ -63,12 +64,13 @@
         (upd1.at[0], u1),
         (rows1, t1s),
         (right1.at[0], r1),
-        (inv1.at[0, half], iv.at[ONE, :, pl.ds(0, B)]),
+        (inv1.at[0], i1),
+        (live1, live1_s),
         (rows2, t2s),
         (upd2, u2),
         (seps, sps),
         (right2, r2),
-        (inv2.at[:, half], iv.at[pl.ds(0, C2), :, pl.ds(0, B)]),
+        (inv2.at[:, half], iv.at[:, :, pl.ds(0, B)]),
     ]
     loads += [(rows1.at[:, pl.ds(d * BD, BD)], t1.at[d]) for d in range(U // BD)]
     loads += [(rows2.at[:, pl.ds(d * BD, BD)], t2.at[d]) for d in range(UT // BD)]
@@ -104,7 +106,13 @@
                 rbuf[f, k] = jnp.zeros((R, B), BF)
             return carry
 
-        lax.fori_loop(0, C2 + 1, zero, 0)
+        lax.fori_loop(0, C2, zero, 0)
+
+    for k in range(6):
+
+        @pl.when(k < 2 * x)
+        def _():
+            rbuf[ONE, k] = jnp.zeros((R, B), BF)
 
     ends = jnp.where(leaf > 0, 1, 0) + jnp.where(leaf < LEAVES - 1, 1, 0)
     pl.semaphore_wait(barrier, 7 + (NY - 1) + (NZ - 1) + ends)
@@ -113,7 +121,7 @@
     for d in range(1, 8):
         rcopy(own_rows, own_rows, g_send.at[d - 1], g_recv.at[d - 1], (leaf, (g + d) % 8)).start()
     def ship(f):
-        src = inv1.at[0, pl.ds(H, H)] if f is ONE else inv2.at[f, pl.ds(H, H)]
+        src = inv2.at[f, pl.ds(H, H)]
         return rcopy(src, iv.at[f, :, pl.ds(B, B)], i_send.at[f], i_recv.at[f], at_x(3 - x))
 
     def each_front(action):
@@ -125,7 +133,6 @@
 
     @pl.when(x < 2)
     def _():
-        ship(ONE).start()
         each_front(lambda f: ship(f).start())
 
     for d in range(1, 8):
@@ -188,15 +195,15 @@
             send(plane(z), i, yz(z + d, y))
         for i in range(3):
             hand(got[i], i)
-        for i in (3, 4):
-            arrived(i)
-            hand(got[i], i)
         arrived(5)
         send(plane(z - 2), 7, yz(z + 1, y))
         send(half_plane(z - 2, 0), 9, yz(z + 2, y))
         arrived(6)
         send(plane(z + 2), 8, yz(z - 1, y))
         send(half_plane(z + 2, 1), 10, yz(z - 2, y))
+        for i in (3, 4):
+            arrived(i)
+            hand(got[i], i)
         for i in (5, 6):
             hand(got[i], i)
         for i in (7, 8, 9, 10):
@@ -294,10 +301,7 @@
 
     def upper(f, live, out):
         from_core(f)
-        if f is ONE:
-            ship(ONE).wait_recv()
-        else:
-            ship(f).wait_recv()
+        ship(f).wait_recv()
         lhs = jnp.concatenate([rbuf[f, 4 + k] for k in range(4)], axis=1)
         both = jnp.dot(lhs, iv[f], preferred_element_type=F32)
         pout[f] = both[:, B:].astype(BF)
@@ -313,7 +317,35 @@
 
     total1 = picked_product(U, LEAVES * B, 0, t1, t1s, top_rows, lambda d: u1[d])
     rbuf[ONE, g] = (r1[...].astype(F32).T - total1).astype(BF)
-    own_sends(ONE)
+
+    def o_x(k, dest):
+        return same(rbuf.at[ONE, 2 * k + c], o_send.at[dest], o_recv.at[k - 1], at_x(dest))
+
+    def o_k(k, core):
+        return same(rbuf.at[ONE, 2 * k + core], ok_send.at[k - 1], ok_recv.at[k - 1], sib)
+
+    def one_sends(act):
+        for dest in range(3):
+            pl.when(dest < x)(lambda: act(o_x(x, dest)))
+        act(ks(ONE, 0, x, c))
+
+    def one_first_hop():
+        for k in range(1, 4):
+
+            @pl.when(k > x)
+            def _():
+                o_x(k, 0).wait_recv()
+                o_k(k, c).start()
+
+    def solve_one():
+        ks(ONE, 0, x, 1 - c).wait_recv()
+        for k in range(1, 4):
+            pl.when(k > x)(lambda: o_k(k, 1 - c).wait_recv())
+        lhs = jnp.concatenate([rbuf[ONE, k] for k in range(8)], axis=1)
+        solved = jnp.dot(lhs, i1[...], preferred_element_type=F32)
+        out_one(jnp.where(lanes < live1_s[0], solved, 0.0))
+
+    one_sends(lambda copy: copy.start())
 
     def s1_x(slot, d):
         return same(s1.at[slot, g], sx_send.at[slot, d - 1], sx_recv.at[slot, d - 1], at_x((x + d) % NX))
@@ -425,22 +457,12 @@
         return out
 
     def body(it, carry):
-        pl.when(it == 1)(lambda: first_hop(ONE))
-        pl.when(jnp.logical_and(it == 2, x >= 2))(lambda: upper(ONE, live1_s[0], out_one))
-        pl.when(jnp.logical_and(it == 3, x < 2))(lambda: lower(ONE, live1_s[0], out_one))
-
-        @pl.when(jnp.logical_and(it == 4, c == 0))
-        def _():
-            s1_neighbours()
-            s1_cross((1,))
-
-        @pl.when(jnp.logical_and(it == 4, c == 1))
-        def _():
-            s1_cross((1,))
-            s1_neighbours()
-
-        pl.when(it == 5)(lambda: s1_cross((0, 2)))
-        pl.when(it == 6)(s1_end)
+        pl.when(it == 3)(one_first_hop)
+        pl.when(it == 4)(solve_one)
+        pl.when(it == 6)(s1_neighbours)
+        pl.when(it == 7)(lambda: s1_cross((1,)))
+        pl.when(it == 10)(lambda: s1_cross((0, 2)))
+        pl.when(it == 11)(s1_end)
 
         def staged(lag, action):
             @pl.when(jnp.logical_and(it >= lag, it < C2 + lag))
@@ -457,11 +479,7 @@
         staged(LAG_D, two_upper)
         staged(LAG_B, parent_part)
         staged(LAG_E, two_lower)
-        @pl.when(it < C2 // 2)
-        def _():
-            top_part(2 * it)
-            top_part(2 * it + 1)
-
+        staged(0, top_part)
         return carry
 
     lax.fori_loop(0, C2 + LAG_E, body, 0)
@@ -486,11 +504,13 @@
 
         return carry
 
-    lax.fori_loop(0, C2 + 1, finish, 0)
+    lax.fori_loop(0, C2, finish, 0)
+    one_sends(lambda copy: copy.wait_send())
+    for k in range(1, 4):
+        pl.when(k > x)(lambda: o_k(k, c).wait_send())
 
     @pl.when(x < 2)
     def _():
-        ship(ONE).wait_send()
         each_front(lambda f: ship(f).wait_send())
 
     def finish_slot(slot):
@@ -527,6 +547,38 @@
         return carry
 
     lax.fori_loop(0, C2, finish_out, 0)
+
+
+PARTS = 6
+
+
+def hand_out(first, second, out1, out2, held, sem_in, sem_out):
+    step = C2 // PARTS
+
+    def part(ref, i):
+        return ref.at[pl.ds(i * step, step)]
+
+    copies = [
+        (
+            pltpu.make_async_copy(part(second, i), part(held, i), sem_in.at[i]),
+            pltpu.make_async_copy(part(held, i), part(out2, i), sem_out.at[i]),
+        )
+        for i in range(PARTS)
+    ]
+    last = held.at[pl.ds(C2, 1)]
+    copies.append(
+        (
+            pltpu.make_async_copy(first, last, sem_in.at[PARTS]),
+            pltpu.make_async_copy(last, out1, sem_out.at[PARTS]),
+        )
+    )
+    for get, _ in copies:
+        get.start()
+    for get, put in copies:
+        get.wait()
+        put.start()
+    for _, put in copies:
+        put.wait()
 
 
 def local(
@@ -537,13 +589,13 @@
     scalar = pl.BlockSpec(memory_space=pltpu.SMEM)
     dma = pltpu.SemaphoreType.DMA
     vm = pltpu.VMEM
-    return pl.pallas_call(
+    first, second = pl.pallas_call(
         kernel,
         out_shape=(
             jax.ShapeDtypeStruct((1, B, R), BF),
             jax.ShapeDtypeStruct((C2, B, R), BF),
         ),
-        in_specs=[anywhere] * 10 + [scalar] * 3,
+        in_specs=[anywhere] * 11 + [scalar] * 2,
         out_specs=(anywhere, anywhere),
         scratch_shapes=[
             vm((B, R), BF),
@@ -558,18 +610,21 @@
             pltpu.SMEM((C2, UT), jnp.int32),
             vm((UP // BD, C2, BD), jnp.int32),
             pltpu.SMEM((C2, UP), jnp.int32),
-            vm((C2 + 1, H, 2 * B), BF),
+            vm((C2, H, 2 * B), BF),
+            vm((S, B), BF),
+            pltpu.SMEM((1,), jnp.int32),
             vm((C2, R, B), F32),
             vm((C2 + 1, 8, R, B), BF),
-            vm((C2 + 1, R, B), BF),
-            vm((C2 + 1, R, B), BF),
+            vm((C2, R, B), BF),
+            vm((C2, R, B), BF),
             vm((3, 8, R, B), BF),
             vm((B, R), BF),
             vm((C2, B, R), BF),
-            dma((26,)), dma((C2 + 1,)),
+            dma((27,)), dma((C2 + 1,)),
             dma((7,)), dma((7,)), dma((11,)), dma((11,)), dma((11,)), dma((11,)),
-            dma((C2 + 1,)), dma((C2 + 1,)), dma((C2 + 1,)), dma((C2 + 1,)), dma((C2 + 1, 2)), dma((C2 + 1, 2)),
-            dma((C2 + 1,)), dma((C2 + 1,)),
+            dma((C2,)), dma((C2,)), dma((C2,)), dma((C2,)), dma((C2 + 1, 2)), dma((C2 + 1, 2)),
+            dma((C2,)), dma((C2,)),
+            dma((3,)), dma((3,)), dma((3,)), dma((3,)),
             dma((2,)), dma((2,)), dma((3, 3)), dma((3, 3)), dma((3, 4)), dma((3, 4)),
         ],
         compiler_params=pltpu.CompilerParams(
@@ -580,8 +635,20 @@
     )(
         top_solution, right_one, update_one.reshape(1, U // BD, BD, B), inverse_one, top_rows_one,
         right_two, update_two.reshape(C2, U // BD, BD, B), inverse_two, top_rows_two, sep_rows,
-        parent, live_one, live_two,
+        live_one, parent, live_two,
     )
+    return pl.pallas_call(
+        hand_out,
+        out_shape=(
+            jax.ShapeDtypeStruct((1, B, R), BF),
+            jax.ShapeDtypeStruct((C2, B, R), BF),
+        ),
+        in_specs=[anywhere] * 2,
+        out_specs=(anywhere, anywhere),
+        scratch_shapes=[pltpu.VMEM((C2 + 1, B, R), BF), dma((PARTS + 1,)), dma((PARTS + 1,))],
+        compiler_params=pltpu.CompilerParams(vmem_limit_bytes=56 * 1024 * 1024),
+        name="hand_out",
+    )(first, second)
 
 
 def solution(mesh):

time: 91.7 us -> 88.9 us (0.969)
  local copies, waits for them, and re-layouts: 3.54 us -> 0 us
  Pallas kernels: 86.5 us -> 87.5 us
    unnamed x2 -> x0, local copies, waits for them, and re-layouts: 3.54 us -> none
    pallas_call x0 -> x1, Pallas kernels: none -> 2 us  [local(): pl.pallas_call(hand_out, out_shape=(jax.ShapeDtypeStruct((1, B, R), BF),...]
    pallas_call x1, Pallas kernels: 86.5 us -> 85.5 us  [local(): pl.pallas_call(kernel, out_shape=(jax.ShapeDtypeStruct((1, B, R), BF), ja...]
where the time goes in v3:
time: 88.9 us; the launch traced here: 88.8 us
  Pallas kernels  87.5 us (98%)
  between operations  1.29 us (1%)
    pallas_call x1, Pallas kernels, local(): pl.pallas_call(kernel, out_shape=(jax.ShapeDtypeStruct((1, B, R), BF), ja...  85.5 us
    pallas_call x1, Pallas kernels, local(): pl.pallas_call(hand_out, out_shape=(jax.ShapeDtypeStruct((1, B, R), BF),...  2 us

profile of v3, /device:TPU:1, one launch (start us, length us, event | category | flops | bytes accessed | tf_op | source)
XLA Modules:
  0.0 88.8 jit_solution(10269672367357025576)
XLA Ops:
  1.3 85.5 %adjoint_solve.1 = (bf16[1,128,256]{2,1,0:T(8,128)(2,1)}, bf16[12,128,256]{2,1,0:T(8,128)(2,1)}) custom-call(bf16[16,256]{1,0:T(8,128)(2,1)} %top.1, bf16[1,128,256]{2,1,0:T(8,128)(2,1)} %right1.1, bf16[1,8,256,128]{3,2,1,0:T(8,128)(2,1)} %bitcast.3, bf16[1,1024,128]{2,1,0:T(8,128)(2,1)} %inv1.1, s32[1,2048]{1,0:T(1,128)} %rows1.1, ...), custom_call_target="tpu_custom_call" | custom-call | flops 20000000000 | bytes 12000000 | tf_op jit(solution)/shard_map/adjoint_solve/pallas_call | solution.py:592
  86.8 2.0 %hand_out.1 = (bf16[1,128,256]{2,1,0:T(8,128)(2,1)}, bf16[12,128,256]{2,1,0:T(8,128)(2,1)}) custom-call(bf16[1,128,256]{2,1,0:T(8,128)(2,1)} %get-tuple-element.4.first, bf16[12,128,256]{2,1,0:T(8,128)(2,1)} %get-tuple-element.5.second), custom_call_target="tpu_custom_call" | custom-call | tf_op jit(solution)/shard_map/hand_out/pallas_call | solution.py:640

commit v4 on v3

--- a/solution.py
+++ b/solution.py
@@ -21,19 +21,19 @@
 NX, NY, NZ = 4, 4, 8
 LEAVES = NY * NZ
 BS = 256
-DELAY = 3
 BD = 256
 
 ONE = C2
 H = S // 2
-LAG_B, LAG_C, LAG_D, LAG_E = 11, 15, 16, 19
+W = 1
+LAG_B, LAG_C, LAG_D, LAG_E = 12, 16, 17, 20
 
 
 def kernel(
     top, right1, upd1, inv1, rows1, right2, upd2, inv2, rows2, seps, live1, parent_s, live2_s,
     out1, out2,
     topb, topT, u1, r1, t1, t1s, u2, r2, t2, t2s, sp, sps, iv, i1, live1_s,
-    acc, rbuf, pbuf, pout, s1, ob1, ob2,
+    acc, cum, rbuf, pbuf, pout, s1, ob1, ob2,
     ld, ldsem_out,
     g_send, g_recv, a_send, a_recv, c_send, c_recv,
     i_send, i_recv, x_send, x_recv, k_send, k_recv, p_send, p_recv,
@@ -173,12 +173,24 @@
     def send(region, i, dev):
         same(region, a_send.at[i], a_recv.at[i], dev).start()
 
-    def gone(got, other):
+    def gone(got):
         for i, region in enumerate(got):
             same(region, a_send.at[i], a_recv.at[i], sib).wait_send()
             same(region, c_send.at[i], c_recv.at[i], sib).wait_send()
+
+    def handed(other):
         for i, region in enumerate(other):
             same(region, c_send.at[i], c_recv.at[i], sib).wait_recv()
+
+    def turn_right():
+        for copy in loads[1:]:
+            copy.wait()
+
+        def one(f, carry):
+            acc[f] = r2[f].astype(F32).T
+            return carry
+
+        lax.fori_loop(0, C2, one, 0)
 
     @pl.when(c == 0)
     def _():
@@ -189,6 +201,7 @@
 
         for i, d in enumerate((1, 3, 2)):
             send(block_at(z, y, 0), i, yz(z, y + d))
+        turn_right()
         for i in range(3):
             arrived(i)
         for i, d in ((5, 2), (6, -2), (3, 1), (4, -1)):
@@ -209,7 +222,7 @@
         for i in (7, 8, 9, 10):
             arrived(i)
             hand(got[i], i)
-        gone(got, pieces1())
+        handed(pieces1())
 
     @pl.when(c == 1)
     def _():
@@ -220,6 +233,7 @@
 
         for i in (4, 3, 5, 2, 6, 1, 7):
             send(block_at(z, y, 1), i - 1, yz(z + i, y))
+        turn_right()
         for i in range(7):
             arrived(i)
         for i, d in ((9, 2), (7, 1), (8, 3)):
@@ -229,10 +243,8 @@
         for i in (7, 8, 9):
             arrived(i)
             hand(got[i], i)
-        gone(got, pieces0())
-
-    for copy in loads[1:]:
-        copy.wait()
+        handed(pieces0())
+
 
     def picked_product(count, pool, front, vec, sca, source, factor):
         nd, ns = count // BD, pool // BS
@@ -244,21 +256,25 @@
             for j in range(1, ns):
                 ends = ends + jnp.where(v >= j * BS, 1, 0)
             passed_at.append(ends)
-        iota = lax.broadcasted_iota(jnp.int32, (BS, BD), 0)
+        iota = lax.broadcasted_iota(jnp.int16, (BS, BD), 0)
         steps = nd + ns - 1
-        pending = []
+        held = None
         for t in range(steps):
             d = jnp.int32(0)
             for ends in passed_at:
                 d = d + jnp.where(ends < t, 1, 0)
             s = t - d
             picks = vec[d, pl.ds(front, 1), :]
-            onehot = jnp.where(iota == picks - s * BS, 1.0, 0.0).astype(BF)
+            onehot = jnp.where(iota == (picks - s * BS).astype(jnp.int16), BF(1), BF(0))
             got = jnp.dot(source(s), onehot, preferred_element_type=F32).astype(BF)
-            pending.append((got, d))
-            while len(pending) > (DELAY if t < steps - 1 else 0):
-                got, d = pending.pop(0)
-                total = total + jnp.dot(got, factor(d), preferred_element_type=F32)
+            if t:
+                keep = jnp.where(d == held[1], 1.0, 0.0)
+                got = got + held[0] * jnp.full((R, BD), keep, F32).astype(BF)
+            cum[t] = got
+            held = (got, d)
+        passed_at.append(steps - 1)
+        for d, last in enumerate(passed_at):
+            total = total + jnp.dot(cum[last], factor(d), preferred_element_type=F32)
         return total
 
     def top_rows(s):
@@ -299,21 +315,30 @@
 
     lanes = lax.broadcasted_iota(jnp.int32, (R, B), 1) + g * B
 
-    def upper(f, live, out):
-        from_core(f)
-        ship(f).wait_recv()
-        lhs = jnp.concatenate([rbuf[f, 4 + k] for k in range(4)], axis=1)
-        both = jnp.dot(lhs, iv[f], preferred_element_type=F32)
-        pout[f] = both[:, B:].astype(BF)
-        ps(f).start()
-        out(jnp.where(lanes < live, both[:, :B], 0.0))
-
-    def lower(f, live, out):
-        from_core(f)
-        lhs = jnp.concatenate([rbuf[f, k] for k in range(4)], axis=1)
-        own = jnp.dot(lhs, iv[f, :, :B], preferred_element_type=F32)
-        ps(f).wait_recv()
-        out(jnp.where(lanes < live, own + pbuf[f].astype(F32), 0.0))
+    def uppers(fronts, outs):
+        for f in fronts:
+            from_core(f)
+            ship(f).wait_recv()
+        both = []
+        for f in fronts:
+            lhs = jnp.concatenate([rbuf[f, 4 + k] for k in range(4)], axis=1)
+            both.append(jnp.dot(lhs, iv[f], preferred_element_type=F32))
+        for f, value in zip(fronts, both):
+            pout[f] = value[:, B:].astype(BF)
+        for f in fronts:
+            ps(f).start()
+        outs(fronts, [value[:, :B] for value in both])
+
+    def lowers(fronts, outs):
+        for f in fronts:
+            from_core(f)
+            ps(f).wait_recv()
+        solved = []
+        for f in fronts:
+            lhs = jnp.concatenate([rbuf[f, k] for k in range(4)], axis=1)
+            own = jnp.dot(lhs, iv[f, :, :B], preferred_element_type=F32)
+            solved.append(own + pbuf[f].astype(F32))
+        outs(fronts, solved)
 
     total1 = picked_product(U, LEAVES * B, 0, t1, t1s, top_rows, lambda d: u1[d])
     rbuf[ONE, g] = (r1[...].astype(F32).T - total1).astype(BF)
@@ -437,108 +462,124 @@
         with_slots((1, 0, 2), body)
 
     def top_part(f):
-        acc[f] = picked_product(UT, LEAVES * B, f, t2, t2s, top_rows, lambda d: u2[f, d])
-
-    def parent_part(f):
-        slot = jnp.clip(parent_s[f] - leaf + 1, 0, 2)
-
-        def parent_rows(s):
-            return jnp.concatenate([s1[slot, 2 * s], s1[slot, 2 * s + 1]], axis=1)
-
-        total = picked_product(UP, S, f, sp, sps, parent_rows, lambda d: u2[f, UT // BD + d])
-        rbuf[f, g] = (r2[f].astype(F32).T - acc[f] - total).astype(BF)
-        own_sends(f)
-
-    def out_two(f):
-        def out(solved):
-            ob2[f] = solved.T.astype(BF)
+        acc[f] = acc[f] - picked_product(UT, LEAVES * B, f, t2, t2s, top_rows, lambda d: u2[f, d])
+
+    def parent_parts(fronts):
+        left = []
+        for f in fronts:
+            slot = jnp.clip(parent_s[f] - leaf + 1, 0, 2)
+
+            def parent_rows(s, slot=slot):
+                return jnp.concatenate([s1[slot, 2 * s], s1[slot, 2 * s + 1]], axis=1)
+
+            total = picked_product(UP, S, f, sp, sps, parent_rows, lambda d, f=f: u2[f, UT // BD + d])
+            left.append((acc[f] - total).astype(BF))
+        for f, value in zip(fronts, left):
+            rbuf[f, g] = value
+        for f in fronts:
+            own_sends(f)
+
+    def out_two(fronts, solved):
+        for f, value in zip(fronts, solved):
+            ob2[f] = jnp.where(lanes < live2_s[f], value, 0.0).T.astype(BF)
+        for f in fronts:
             pltpu.make_async_copy(ob2.at[f], out2.at[f], ldsem_out.at[f]).start()
 
-        return out
+    def finish(fronts):
+        f, = fronts
+        ks(f, 0, x, c).wait_send()
+
+        @pl.when(sends)
+        def _():
+            xs(f, x, twin).wait_send()
+
+        @pl.when(gets)
+        def _():
+            ks(f, 1, twin, c).wait_send()
+
+        @pl.when(x >= 2)
+        def _():
+            ps(f).wait_send()
+
+
+    def early_sends_gone():
+        pl.when(c == 0)(lambda: gone(pieces0()))
+        pl.when(c == 1)(lambda: gone(pieces1()))
+
+    def later_sends_gone():
+        for d in range(1, 8):
+            rcopy(own_rows, own_rows, g_send.at[d - 1], g_recv.at[d - 1], (leaf, (g + d) % 8)).wait_send()
+
+        one_sends(lambda copy: copy.wait_send())
+        for k in range(1, 4):
+            pl.when(k > x)(lambda: o_k(k, c).wait_send())
+
+        @pl.when(x < 2)
+        def _():
+            each_front(lambda f: ship(f).wait_send())
+
+        def finish_slot(slot):
+            def over_x():
+                for d in range(1, 4):
+                    s1_x(slot, d).wait_send()
+
+            if slot == 1:
+                over_x()
+            else:
+                pl.when(c == 0)(over_x)
+            for k in range(NX):
+                s1_k(slot, k, c).wait_send()
+
+        @pl.when(c == 1)
+        def _():
+            for d in range(1, 4):
+                s1_relay(d, lambda copy: copy.wait_send())
+
+        with_slots((0, 1, 2), finish_slot)
+
+        @pl.when(leaf < LEAVES - 1)
+        def _():
+            s1_up().wait_send()
+
+        @pl.when(leaf > 0)
+        def _():
+            s1_down().wait_send()
+
 
     def body(it, carry):
         pl.when(it == 3)(one_first_hop)
         pl.when(it == 4)(solve_one)
-        pl.when(it == 6)(s1_neighbours)
-        pl.when(it == 7)(lambda: s1_cross((1,)))
-        pl.when(it == 10)(lambda: s1_cross((0, 2)))
-        pl.when(it == 11)(s1_end)
+        pl.when(it == 7)(s1_neighbours)
+        pl.when(it == 8)(lambda: s1_cross((1,)))
+        pl.when(it == 11)(lambda: s1_cross((0, 2)))
+        pl.when(it == 12)(s1_end)
 
         def staged(lag, action):
-            @pl.when(jnp.logical_and(it >= lag, it < C2 + lag))
+            @pl.when(jnp.logical_and(it >= lag, it < C2 // W + lag))
             def _():
-                action(it - lag)
-
-        def two_upper(f):
-            pl.when(x >= 2)(lambda: upper(f, live2_s[f], out_two(f)))
-
-        def two_lower(f):
-            pl.when(x < 2)(lambda: lower(f, live2_s[f], out_two(f)))
-
-        staged(LAG_C, first_hop)
+                action([(it - lag) * W + i for i in range(W)])
+
+        def first_hops(fronts):
+            for f in fronts:
+                first_hop(f)
+
+        def two_upper(fronts):
+            pl.when(x >= 2)(lambda: uppers(fronts, out_two))
+
+        def two_lower(fronts):
+            pl.when(x < 2)(lambda: lowers(fronts, out_two))
+
+        staged(LAG_C, first_hops)
         staged(LAG_D, two_upper)
-        staged(LAG_B, parent_part)
+        staged(LAG_B, parent_parts)
         staged(LAG_E, two_lower)
-        staged(0, top_part)
+        staged(LAG_E + 1, finish)
+        pl.when(it == LAG_B + 2)(early_sends_gone)
+        pl.when(it == LAG_C + 2)(later_sends_gone)
+        pl.when(it < C2)(lambda: top_part(it))
         return carry
 
-    lax.fori_loop(0, C2 + LAG_E, body, 0)
-
-    for d in range(1, 8):
-        rcopy(own_rows, own_rows, g_send.at[d - 1], g_recv.at[d - 1], (leaf, (g + d) % 8)).wait_send()
-
-    def finish(f, carry):
-        ks(f, 0, x, c).wait_send()
-
-        @pl.when(sends)
-        def _():
-            xs(f, x, twin).wait_send()
-
-        @pl.when(gets)
-        def _():
-            ks(f, 1, twin, c).wait_send()
-
-        @pl.when(x >= 2)
-        def _():
-            ps(f).wait_send()
-
-        return carry
-
-    lax.fori_loop(0, C2, finish, 0)
-    one_sends(lambda copy: copy.wait_send())
-    for k in range(1, 4):
-        pl.when(k > x)(lambda: o_k(k, c).wait_send())
-
-    @pl.when(x < 2)
-    def _():
-        each_front(lambda f: ship(f).wait_send())
-
-    def finish_slot(slot):
-        def over_x():
-            for d in range(1, 4):
-                s1_x(slot, d).wait_send()
-
-        if slot == 1:
-            over_x()
-        else:
-            pl.when(c == 0)(over_x)
-        for k in range(NX):
-            s1_k(slot, k, c).wait_send()
-
-    @pl.when(c == 1)
-    def _():
-        for d in range(1, 4):
-            s1_relay(d, lambda copy: copy.wait_send())
-
-    with_slots((0, 1, 2), finish_slot)
-
-    @pl.when(leaf < LEAVES - 1)
-    def _():
-        s1_up().wait_send()
-
-    @pl.when(leaf > 0)
-    def _():
-        s1_down().wait_send()
+    lax.fori_loop(0, C2 + LAG_E + 1, body, 0)
 
     pltpu.make_async_copy(ob1, out1.at[0], ldsem_out.at[C2]).wait()
 
@@ -614,6 +655,7 @@
             vm((S, B), BF),
             pltpu.SMEM((1,), jnp.int32),
             vm((C2, R, B), F32),
+            vm((U // BD + LEAVES * B // BS, R, BD), BF),
             vm((C2 + 1, 8, R, B), BF),
             vm((C2, R, B), BF),
             vm((C2, R, B), BF),

time: 88.9 us -> 86.7 us (0.975)
  Pallas kernels: 87.5 us -> 85.3 us
    pallas_call x1, Pallas kernels: 85.5 us -> 83.3 us  [local(): pl.pallas_call(kernel, out_shape=(jax.ShapeDtypeStruct((1, B, R), BF), ja...]
where the time goes in v4:
time: 86.7 us; the launch traced here: 86.6 us
  Pallas kernels  85.3 us (98%)
  between operations  1.29 us (1%)
    pallas_call x1, Pallas kernels, local(): pl.pallas_call(kernel, out_shape=(jax.ShapeDtypeStruct((1, B, R), BF), ja...  83.3 us
    pallas_call x1, Pallas kernels, local(): pl.pallas_call(hand_out, out_shape=(jax.ShapeDtypeStruct((1, B, R), BF),...  2 us

profile of v4, /device:TPU:1, one launch (start us, length us, event | category | flops | bytes accessed | tf_op | source)
XLA Modules:
  0.0 86.6 jit_solution(17527286465824728609)
XLA Ops:
  1.3 83.3 %adjoint_solve.1 = (bf16[1,128,256]{2,1,0:T(8,128)(2,1)}, bf16[12,128,256]{2,1,0:T(8,128)(2,1)}) custom-call(bf16[16,256]{1,0:T(8,128)(2,1)} %top.1, bf16[1,128,256]{2,1,0:T(8,128)(2,1)} %right1.1, bf16[1,8,256,128]{3,2,1,0:T(8,128)(2,1)} %bitcast.3, bf16[1,1024,128]{2,1,0:T(8,128)(2,1)} %inv1.1, s32[1,2048]{1,0:T(1,128)} %rows1.1, ...), custom_call_target="tpu_custom_call" | custom-call | flops 20000000000 | bytes 12000000 | tf_op jit(solution)/shard_map/adjoint_solve/pallas_call | solution.py:633
  84.6 2.0 %hand_out.1 = (bf16[1,128,256]{2,1,0:T(8,128)(2,1)}, bf16[12,128,256]{2,1,0:T(8,128)(2,1)}) custom-call(bf16[1,128,256]{2,1,0:T(8,128)(2,1)} %get-tuple-element.4.first, bf16[12,128,256]{2,1,0:T(8,128)(2,1)} %get-tuple-element.5.second), custom_call_target="tpu_custom_call" | custom-call | tf_op jit(solution)/shard_map/hand_out/pallas_call | solution.py:682

commit v5 on v4

--- a/solution.py
+++ b/solution.py
@@ -26,7 +26,7 @@
 ONE = C2
 H = S // 2
 W = 1
-LAG_B, LAG_C, LAG_D, LAG_E = 12, 16, 17, 20
+LAG_B, LAG_C, LAG_D, LAG_E = 13, 17, 18, 21
 
 
 def kernel(
@@ -547,12 +547,12 @@
 
 
     def body(it, carry):
-        pl.when(it == 3)(one_first_hop)
-        pl.when(it == 4)(solve_one)
-        pl.when(it == 7)(s1_neighbours)
-        pl.when(it == 8)(lambda: s1_cross((1,)))
-        pl.when(it == 11)(lambda: s1_cross((0, 2)))
-        pl.when(it == 12)(s1_end)
+        pl.when(it == 4)(one_first_hop)
+        pl.when(it == 5)(solve_one)
+        pl.when(it == 8)(s1_neighbours)
+        pl.when(it == 9)(lambda: s1_cross((1,)))
+        pl.when(it == 12)(lambda: s1_cross((0, 2)))
+        pl.when(it == 13)(s1_end)
 
         def staged(lag, action):
             @pl.when(jnp.logical_and(it >= lag, it < C2 // W + lag))

time: 86.7 us -> 86.4 us (level)
  no operation moved by 1% of the time
where the time goes in v5:
time: 86.4 us; the launch traced here: 86.1 us
  Pallas kernels  84.8 us (98%)
  between operations  1.29 us (1%)
    pallas_call x1, Pallas kernels, local(): pl.pallas_call(kernel, out_shape=(jax.ShapeDtypeStruct((1, B, R), BF), ja...  82.8 us
    pallas_call x1, Pallas kernels, local(): pl.pallas_call(hand_out, out_shape=(jax.ShapeDtypeStruct((1, B, R), BF),...  2 us

profile of v5, /device:TPU:1, one launch (start us, length us, event | category | flops | bytes accessed | tf_op | source)
XLA Modules:
  0.0 86.1 jit_solution(17702766708747470117)
XLA Ops:
  1.3 82.8 %adjoint_solve.1 = (bf16[1,128,256]{2,1,0:T(8,128)(2,1)}, bf16[12,128,256]{2,1,0:T(8,128)(2,1)}) custom-call(bf16[16,256]{1,0:T(8,128)(2,1)} %top.1, bf16[1,128,256]{2,1,0:T(8,128)(2,1)} %right1.1, bf16[1,8,256,128]{3,2,1,0:T(8,128)(2,1)} %bitcast.3, bf16[1,1024,128]{2,1,0:T(8,128)(2,1)} %inv1.1, s32[1,2048]{1,0:T(1,128)} %rows1.1, ...), custom_call_target="tpu_custom_call" | custom-call | flops 20000000000 | bytes 12000000 | tf_op jit(solution)/shard_map/adjoint_solve/pallas_call | solution.py:633
  84.1 2.0 %hand_out.1 = (bf16[1,128,256]{2,1,0:T(8,128)(2,1)}, bf16[12,128,256]{2,1,0:T(8,128)(2,1)}) custom-call(bf16[1,128,256]{2,1,0:T(8,128)(2,1)} %get-tuple-element.4.first, bf16[12,128,256]{2,1,0:T(8,128)(2,1)} %get-tuple-element.5.second), custom_call_target="tpu_custom_call" | custom-call | tf_op jit(solution)/shard_map/hand_out/pallas_call | solution.py:682
